TPU v7x, 256 devices: a whole 4x4x8 slice. The times are simulated.
256 devices in a mesh: seq: 8 (over y, core), ep: 32 (over x, z).
Axes of the slice: x: 4, y: 4, z: 8, core: 2. Of those that a mesh axis runs over, the one named last changes fastest.
Arguments:
- entering: bfloat16 [32, 32, 7168], P('ep', 'seq'), may hold values from -6 to 6
- moe_gain: float32 [7168], replicated, may hold values from 0.1 to 1.9
- expert_ids: int32 [32, 32, 8], P('ep'), may hold values from 0 to 31, all different within a row; in each aligned block of 4 rows (0 to 3, 4 to 7, ..., all dimensions but the last counted through in order) at most 2 rows name the same one
- gate_weights: float32 [32, 32, 8], P('ep'), may hold values from 0.05 to 0.5
- w_gate: bfloat16 [32, 7168, 2048], P('ep', None, 'seq'), may hold values from -0.0625 to 0.0625
- w_up: bfloat16 [32, 7168, 2048], P('ep', None, 'seq'), may hold values from -0.0625 to 0.0625
- w_down: bfloat16 [32, 2048, 7168], P('ep', 'seq'), may hold values from -0.125 to 0.125
- w_latent: bfloat16 [7168, 512], P('seq'), may hold values from -0.0625 to 0.0625
- w_rope: bfloat16 [64, 7168], P(None, 'seq'), may hold values from -0.0625 to 0.0625
- latent_gain: float32 [512], replicated, may hold values from 0.1 to 1.9
- prefix_len: int32 [32], P('ep'), may hold values from 128 to 1024, as said below
- cache_latent: bfloat16 [32, 1024, 512], P('ep', 'seq'), may hold values from -4 to 4
- cache_rope: bfloat16 [32, 64, 1024], P('ep', None, 'seq'), may hold values from -4 to 4
- query_latent: bfloat16 [32, 32, 65536], P('ep', 'seq'), may hold values from -7 to 7
- query_rope: bfloat16 [32, 32, 8192], P('ep', 'seq'), may hold values from -32 to 32
Outputs:
- layer_out: bfloat16 [32, 32, 7168], P('ep', None, 'seq')
- attention: bfloat16 [32, 32, 65536], P('ep', 'seq')
Inputs may be any that keep to these rules, and one draw needn't show every extreme that they name: `expert_ids`: in each aligned block of 4 rows (one document's new tokens on one index of seq) no expert is named by more than 2 tokens, and in some blocks one is named by exactly 2. Each token names 8 different experts. `prefix_len`: some document has all 1024 positions cached.
All inputs are finite; a program needn't handle non-finite values.
Results may differ from a plain program's by a relative error of at most 0.018.
Values may be sent and summed in bfloat16 or wider, within the bound.
A program may use at most 128 MiB of HBM per device.

v0:
```python
import jax
import jax.numpy as jnp
from jax import lax
from jax.sharding import PartitionSpec as P

softmax_scale = 192 ** (-0.5)
rope_base = 10000.0


def rms_rows(values, gain):
    mean_sq = jnp.mean(values * values, axis=-1, keepdims=True)
    return values * lax.rsqrt(mean_sq + 1e-06) * gain


def rotate_pairs(values, positions):
    half = values.shape[-1] // 2
    steps = jnp.arange(half, dtype=jnp.float32) * 2.0 / values.shape[-1]
    freqs = rope_base ** (-steps)
    angle = positions.astype(jnp.float32)[:, None] * freqs[None, :]
    first = values[:, :half]
    second = values[:, half:]
    cosine = jnp.cos(angle)
    sine = jnp.sin(angle)
    return jnp.concatenate(
        [first * cosine - second * sine, second * cosine + first * sine], axis=-1
    )


def score_block(query_lat, query_rot, key_lat, key_rot_cols):
    lat_part = jnp.dot(query_lat, key_lat.T, preferred_element_type=jnp.float32)
    rot_part = jnp.dot(query_rot, key_rot_cols, preferred_element_type=jnp.float32)
    return (lat_part + rot_part) * softmax_scale


def block_slots(routes, experts, capacity):
    same = (routes[:, :, None, None] == routes[None, None, :, :]).any(axis=3)
    order = jnp.arange(routes.shape[0], dtype=jnp.int32)
    earlier = order[None, :] < order[:, None]
    slots = jnp.sum((same & earlier[:, None, :]).astype(jnp.int32), axis=2)
    return routes * capacity + slots


def expert_terms(rows, gate_matrix, up_matrix, down_matrix):
    gate = jnp.dot(rows, gate_matrix, preferred_element_type=jnp.float32)
    upper = jnp.dot(rows, up_matrix, preferred_element_type=jnp.float32)
    hidden = (jax.nn.silu(gate) * upper).astype(jnp.bfloat16)
    return jnp.dot(hidden, down_matrix, preferred_element_type=jnp.float32)


def local(
    entering,
    moe_gain,
    expert_ids,
    gate_weights,
    w_gate,
    w_up,
    w_down,
    w_latent,
    w_rope,
    latent_gain,
    prefix_len,
    cache_latent,
    cache_rope,
    query_latent,
    query_rope,
):
    seq_count = lax.axis_size("seq")
    seq_place = lax.axis_index("seq")
    experts = lax.axis_size("ep")
    own_entering = entering[0]
    new_dev, width = own_entering.shape
    new = new_dev * seq_count
    capacity = 2
    prefix = prefix_len[0]
    heads = query_latent.shape[2] // cache_latent.shape[2]
    lat_width = cache_latent.shape[2]
    rot_width = cache_rope.shape[1]

    routes = lax.dynamic_slice_in_dim(expert_ids[0], seq_place * new_dev, new_dev, 0)
    gates = lax.dynamic_slice_in_dim(gate_weights[0], seq_place * new_dev, new_dev, 0)
    normed = rms_rows(own_entering.astype(jnp.float32), moe_gain).astype(jnp.bfloat16)
    targets = block_slots(routes, experts, capacity)
    total_slots = experts * capacity
    hits = targets[:, :, None] == jnp.arange(total_slots, dtype=jnp.int32)[None, None, :]
    placement = jnp.any(hits, axis=1).astype(jnp.bfloat16)
    gate_rows = jnp.sum(jnp.where(hits, gates[:, :, None], 0.0), axis=1)
    outgoing = jnp.dot(placement.T, normed, preferred_element_type=jnp.float32)
    outgoing = outgoing.astype(jnp.bfloat16).reshape(experts, capacity, width)
    arrived = lax.all_to_all(outgoing, "ep", split_axis=0, concat_axis=0, tiled=True)
    rows = lax.all_gather(arrived.reshape(total_slots, width), "seq", axis=0, tiled=True)

    older_lat = lax.all_gather(cache_latent[0], "seq", axis=0, tiled=True)
    older_rot = lax.all_gather(cache_rope[0], "seq", axis=1, tiled=True)
    query_lat = query_latent[0].reshape(new_dev * heads, lat_width)
    query_rot = query_rope[0].reshape(new_dev * heads, rot_width)
    older = score_block(query_lat, query_rot, older_lat, older_rot)
    cache_ok = (jnp.arange(older_lat.shape[0], dtype=jnp.int32) < prefix)[None, :]
    older = jnp.where(cache_ok, older, -jnp.inf)
    older_high = jnp.max(older, axis=1)
    older_weights = jnp.exp(older - older_high[:, None])
    older_total = jnp.sum(older_weights, axis=1)
    older_sum = jnp.dot(
        older_weights.astype(jnp.bfloat16), older_lat, preferred_element_type=jnp.float32
    )

    terms = expert_terms(rows, w_gate[0], w_up[0], w_down[0]).astype(jnp.bfloat16)
    summed = lax.psum_scatter(terms, "seq", scatter_dimension=0, tiled=True)
    summed = summed.reshape(experts, capacity, width)
    returned = lax.all_to_all(summed, "ep", split_axis=0, concat_axis=0, tiled=True)
    weighted = jnp.dot(
        gate_rows,
        returned.reshape(total_slots, width).astype(jnp.float32),
        precision=lax.Precision.HIGHEST,
    )
    layer_own = (own_entering.astype(jnp.float32) + weighted).astype(jnp.bfloat16)
    layer = lax.all_to_all(layer_own, "seq", split_axis=1, concat_axis=0, tiled=True)
    latent_part = jnp.dot(layer, w_latent, preferred_element_type=jnp.float32)
    rope_part = lax.dot_general(
        layer, w_rope, (((1,), (1,)), ((), ())), preferred_element_type=jnp.float32
    )
    raw = lax.psum(jnp.concatenate([latent_part, rope_part], axis=1), "seq")
    fresh_lat = rms_rows(raw[:, :lat_width], latent_gain).astype(jnp.bfloat16)
    positions = prefix + jnp.arange(new, dtype=jnp.int32)
    fresh_rot = rotate_pairs(raw[:, lat_width:], positions).astype(jnp.bfloat16)

    fresh = score_block(query_lat, query_rot, fresh_lat, fresh_rot.T)
    query_place = seq_place * new_dev + jnp.arange(new_dev * heads, dtype=jnp.int32) // heads
    fresh_ok = jnp.arange(new, dtype=jnp.int32)[None, :] <= query_place[:, None]
    fresh = jnp.where(fresh_ok, fresh, -jnp.inf)
    highest = jnp.maximum(older_high, jnp.max(fresh, axis=1))
    scale = jnp.exp(older_high - highest)
    fresh_weights = jnp.exp(fresh - highest[:, None])
    total = older_total * scale + jnp.sum(fresh_weights, axis=1)
    gathered = older_sum * scale[:, None] + jnp.dot(
        fresh_weights.astype(jnp.bfloat16), fresh_lat, preferred_element_type=jnp.float32
    )
    output = (gathered / total[:, None]).astype(jnp.bfloat16).reshape(new_dev, heads * lat_width)
    return (layer[None], output[None])


def solution(mesh):
    placed = (
        P("ep", "seq", None),
        P(),
        P("ep", None, None),
        P("ep", None, None),
        P("ep", None, "seq"),
        P("ep", None, "seq"),
        P("ep", "seq", None),
        P("seq", None),
        P(None, "seq"),
        P(),
        P("ep"),
        P("ep", "seq", None),
        P("ep", None, "seq"),
        P("ep", "seq", None),
        P("ep", "seq", None),
    )
    return jax.shard_map(
        local,
        mesh=mesh,
        in_specs=placed,
        out_specs=(P("ep", None, "seq"), P("ep", "seq", None)),
        check_vma=False,
    )
```

profile of v0, /device:TPU:1, one launch (start us, length us, event | category | flops | bytes accessed | tf_op | source)
XLA Modules:
  0.0 291.2 jit_solution(7209616721143365374)
XLA Ops:
  7.2 0.0 copy-start
  7.2 0.0 all-gather.5.cloned.1.call-start
  7.2 0.8 constant_dynamic-slice_fusion.1
  8.1 0.1 copy.23
  8.2 0.4 compare_reduce_fusion
  8.6 0.1 convert_reduce_fusion
  8.7 0.1 fusion.47
  8.8 1.0 fusion.28
  9.8 1.3 convolution_convert_fusion.1
  11.1 0.3 reshape.118
  11.4 33.6 %all_to_all.29 = bf16[32,2,7168]{2,1,0:T(2,128)(2,1)S(1)} all-to-all(bf16[32,2,7168]{2,1,0:T(2,128)(2,1)S(1)} %reshape.118), channel_id=1, replica_groups=mesh['seq'=8,'ep'=32] {'ep'}, dimensions={0} | all-to-all | bytes 1835008 | tf_op jit(solution)/shard_map/all_to_all | solution.py:89
  45.0 1.3 reshape.119
  46.3 0.0 all-gather.5.cloned.1.call-update
  46.3 0.0 reduce-scatter.2.cloned.1.call-start
  46.4 49.3 %all-gather.5.cloned.1.call-done = bf16[512,7168]{1,0:T(8,128)(2,1)} async-done(((bf16[64,7168]{1,0:T(8,128)(2,1)}), bf16[512,7168]{1,0:T(8,128)(2,1)}) %all-gather.5.cloned.1.call-update) | async-done | bytes 7340048 | tf_op jit(solution)/shard_map/all_gather | solution.py:90
  95.7 6.2 %fusion.4 = f32[512,256]{1,0:T(8,128)S(1)} fusion(bf16[512,7168]{1,0:T(8,128)(2,1)} %all-gather.5.cloned.1.call-done, bf16[1,7168,256]{2,1,0:T(8,128)(2,1)} %param.19), kind=kOutput, calls=%fused_computation.7 | convolution fusion | flops 1879048192 | bytes 11534336 | tf_op jit(solution)/shard_map/dot_general | solution.py:44
  101.9 16.0 %convolution_convert_fusion = bf16[512,7168]{1,0:T(8,128)(2,1)} fusion(bf16[1,256,7168]{2,1,0:T(8,128)(2,1)} %param.21, bf16[512,7168]{1,0:T(8,128)(2,1)} %all-gather.5.cloned.1.call-done, bf16[1,7168,256]{2,1,0:T(8,128)(2,1)} %param.20, f32[512,256]{1,0:T(8,128)S(1)} %fusion.4), kind=kOutput, calls=%fused_computation | convolution fusion | flops 3762552832 | bytes 22544384 | tf_op jit(solution)/shard_map/dot_general | solution.py:47
  117.9 0.0 reduce-scatter.2.cloned.1.call-update
  117.9 0.0 copy-start.7
  117.9 0.0 copy-start.5
  117.9 0.0 copy-start.2
  118.0 0.0 copy-start.6
  118.0 49.3 %reduce-scatter.2.cloned.1.call-done = bf16[64,7168]{1,0:T(8,128)(2,1)} async-done(((bf16[512,7168]{1,0:T(8,128)(2,1)}), bf16[64,7168]{1,0:T(8,128)(2,1)}) %reduce-scatter.2.cloned.1.call-update) | async-done | bytes 917520 | tf_op jit(solution)/shard_map/reduce_scatter | solution.py:107
  167.2 3.1 %reshape.120 = bf16[32,2,7168]{2,1,0:T(2,128)(2,1)} reshape(bf16[64,7168]{1,0:T(8,128)(2,1)} %reduce-scatter.2.cloned.1.call-done) | data formatting | bytes 1835008 | tf_op jit(solution)/shard_map/reshape | solution.py:108
  170.3 9.7 %all-to-all-start.1 = ((bf16[32,2,7168]{2,1,0:T(2,128)(2,1)}), bf16[32,2,7168]{2,1,0:T(2,128)(2,1)S(1)}, u32[]{:S(2)}, u32[]{:S(2)}) async-start(bf16[32,2,7168]{2,1,0:T(2,128)(2,1)} %reshape.120), calls=%async_computation.2 | async-start | bytes 1835008 | tf_op jit(solution)/shard_map/all_to_all | solution.py:109
  180.0 0.2 all-gather.7.cloned.1.call-start
  180.2 0.5 all-gather.7.cloned.1.call-update
  180.7 0.0 copy-done.7
  180.7 0.1 constant_dynamic-slice_fusion
  180.8 0.1 copy.24
  180.9 0.0 copy-done.5
  180.9 0.2 reshape_squeeze.7
  181.1 0.0 copy-start.1
  181.1 0.4 reshape_squeeze.6
  182.2 12.7 %all-gather.1 = bf16[1,64,1024]{2,1,0:T(8,128)(2,1)S(1)} all-gather(bf16[1,64,128]{2,1,0:T(8,128)(2,1)S(1)} %copy-done.6), channel_id=3, replica_groups=mesh['seq'=8,'ep'=32] {'seq'}, dimensions={2}, use_global_device_ids=true | all-gather | bytes 147456 | tf_op jit(solution)/shard_map/all_gather | solution.py:93
  194.8 0.6 negate_power_fusion
  195.4 0.5 add_convert_fusion
  196.0 0.1 select_reduce_fusion
  196.1 1.8 fusion.26
  197.8 4.2 %all-to-all-done.1 = bf16[32,2,7168]{2,1,0:T(2,128)(2,1)S(1)} async-done(((bf16[32,2,7168]{2,1,0:T(2,128)(2,1)}), bf16[32,2,7168]{2,1,0:T(2,128)(2,1)S(1)}, u32[]{:S(2)}, u32[]{:S(2)}) %all-to-all-start.1) | async-done | bytes 917536 | tf_op jit(solution)/shard_map/all_to_all | solution.py:109
  202.0 0.3 reshape.121
  202.3 0.0 copy-done.3
  202.4 1.1 fusion
  203.5 8.9 %all-to-all-start.2 = ((bf16[4,8,896]{2,0,1:T(4,128)(2,1)}), bf16[4,8,896]{2,0,1:T(4,128)(2,1)}, u32[]{:S(2)}, u32[]{:S(2)}) async-start(bf16[4,8,896]{2,0,1:T(4,128)(2,1)} %bitcast.7), calls=%async_computation.3 | async-start | bytes 114688 | tf_op jit(solution)/shard_map/all_to_all | solution.py:116
  212.4 0.0 all-gather.7.cloned.1.call-done
  212.4 2.8 fusion.58
  215.2 2.1 all-to-all-done.2
  217.3 1.5 all_to_all.25
  218.8 1.1 fusion.61
  219.8 0.0 copy-done
  219.9 1.1 fusion.60
  220.9 0.7 pad_maximum_fusion
  221.6 0.0 all-reduce.2.cloned.1.call-update
  221.6 0.5 fusion.6
  222.1 1.5 broadcast_in_dim.34
  223.5 53.4 %all-reduce.2.cloned.1.call-done = f32[32,576]{1,0:T(8,128)} async-done(((f32[32,576]{1,0:T(8,128)}), f32[32,576]{1,0:T(8,128)}) %all-reduce.2.cloned.1.call-update) | async-done | bytes 73744 | tf_op jit(solution)/shard_map/psum | solution.py:121
  276.9 1.0 multiply_reduce_fusion
  278.0 1.1 fusion.57
  279.0 1.0 fusion.44
  280.0 1.1 fusion.59
  281.2 2.0 convolution_multiply_fusion
  283.2 0.0 copy-done.4
  283.2 0.3 fusion.9
  283.5 1.2 broadcast_in_dim_reshape.3
  (17 shorter events, 0.1 us)
Async XLA Ops:
  7.2 212.7 %copy-start = (bf16[896,512]{1,0:T(8,128)(2,1)S(1)}, bf16[896,512]{1,0:T(8,128)(2,1)}, u32[]{:S(2)}) copy-start(bf16[896,512]{1,0:T(8,128)(2,1)} %param.22) | copy-start | bytes 2752516
  7.2 88.5 %all-gather.5.cloned.1.call-start = ((), (), s32[]{:S(2)}) async-start(), calls=%async_computation.4 | async-start | bytes 8257536 | tf_op jit(solution)/shard_map/all_gather | solution.py:90
  46.3 120.9 %reduce-scatter.2.cloned.1.call-start = ((), (), s32[]{:S(2)}) async-start(), calls=%async_computation.5 | async-start | bytes 8257536 | tf_op jit(solution)/shard_map/reduce_scatter | solution.py:107
  117.9 62.8 %copy-start.7 = (f32[1,32,8]{1,2,0:T(8,128)S(1)}, f32[1,32,8]{1,2,0:T(8,128)}, u32[]{:S(2)}) copy-start(f32[1,32,8]{1,2,0:T(8,128)} %param.18) | copy-start | bytes 3076
  117.9 63.0 %copy-start.5 = (bf16[1,4,8192]{2,1,0:T(4,128)(2,1)S(1)}, bf16[1,4,8192]{2,1,0:T(4,128)(2,1)}, u32[]{:S(2)}) copy-start(bf16[1,4,8192]{2,1,0:T(4,128)(2,1)} %param.29) | copy-start | bytes 196612
  117.9 63.1 %copy-start.2 = (bf16[1,4,65536]{2,1,0:T(4,128)(2,1)S(1)}, bf16[1,4,65536]{2,1,0:T(4,128)(2,1)}, u32[]{:S(2)}) copy-start(bf16[1,4,65536]{2,1,0:T(4,128)(2,1)} %param.28) | copy-start | bytes 1572868
  118.0 64.2 %copy-start.6 = (bf16[1,64,128]{2,1,0:T(8,128)(2,1)S(1)}, bf16[1,64,128]{2,1,0:T(8,128)(2,1)}, u32[]{:S(2)}) copy-start(bf16[1,64,128]{2,1,0:T(8,128)(2,1)} %param.27) | copy-start | bytes 49156
  170.3 32.1 %copy-start.3 = (bf16[1,4,7168]{2,1,0:T(4,128)(2,1)S(1)}, bf16[1,4,7168]{2,1,0:T(4,128)(2,1)}, u32[]{:S(2)}) copy-start(bf16[1,4,7168]{2,1,0:T(4,128)(2,1)} %param.15) | copy-start | bytes 172036
  170.3 31.7 %all-to-all-start.1 = ((bf16[32,2,7168]{2,1,0:T(2,128)(2,1)}), bf16[32,2,7168]{2,1,0:T(2,128)(2,1)S(1)}, u32[]{:S(2)}, u32[]{:S(2)}) async-start(bf16[32,2,7168]{2,1,0:T(2,128)(2,1)} %reshape.120), calls=%async_computation.2 | async-start | bytes 1835008 | tf_op jit(solution)/shard_map/all_to_all | solution.py:109
  180.0 32.4 %all-gather.7.cloned.1.call-start = ((), (), s32[]{:S(2)}) async-start(), calls=%async_computation.7 | async-start | bytes 1179648 | tf_op jit(solution)/shard_map/all_gather | solution.py:92
  181.1 16.8 %copy-start.1 = (bf16[512,64]{1,0:T(8,128)(2,1)}, bf16[512,64]{1,0:T(8,128)(2,1)S(1)}, u32[]{:S(2)}) copy-start(bf16[512,64]{1,0:T(8,128)(2,1)S(1)} %reshape_squeeze.7) | copy-start | bytes 196612
  203.5 13.8 %all-to-all-start.2 = ((bf16[4,8,896]{2,0,1:T(4,128)(2,1)}), bf16[4,8,896]{2,0,1:T(4,128)(2,1)}, u32[]{:S(2)}, u32[]{:S(2)}) async-start(bf16[4,8,896]{2,0,1:T(4,128)(2,1)} %bitcast.7), calls=%async_computation.3 | async-start | bytes 114688 | tf_op jit(solution)/shard_map/all_to_all | solution.py:116
  212.4 65.6 %copy-start.8 = (f32[512]{0:T(512)S(1)}, f32[512]{0:T(512)}, u32[]{:S(2)}) copy-start(f32[512]{0:T(512)} %param.24) | copy-start | bytes 6148
  212.4 64.5 %all-reduce.2.cloned.1.call-start = ((), (), s32[]{:S(2)}) async-start(), calls=%async_computation.6 | async-start | bytes 163840 | tf_op jit(solution)/shard_map/psum | solution.py:121
  276.9 6.3 %copy-start.4 = (f32[32,576]{1,0:T(8,128)S(1)}, f32[32,576]{1,0:T(8,128)}, u32[]{:S(2)}) copy-start(f32[32,576]{1,0:T(8,128)} %all-reduce.2.cloned.1.call-done) | copy-start | bytes 221188
Sparse Core Ops, SparseCore 0:
  46.5 49.1 all-gather.4
  118.0 49.1 reduce-scatter.1
  182.7 26.2 all-gather.6
  221.7 55.1 all-reduce.1
where the time goes:
time: 292 us; the launch traced here: 291 us
  waiting for transfers between devices  159 us (54%)
  blocking collectives  46.3 us (16%)
  matrix products  35.8 us (12%)
  starting transfers between devices  18.9 us (6%)
  between operations  14.6 us (5%)
  local copies, waits for them, and re-layouts  10.8 us (4%)
  other arithmetic  6.02 us (2%)
    psum x1, waiting for transfers between devices, local(): raw = lax.psum(jnp.concatenate([latent_part, rope_part], axis=1), 'seq')  53.4 us
    all_gather x1, waiting for transfers between devices, local(): lax.all_gather(arrived.reshape(total_slots, width), 'seq', axis=0, tiled=...  49.3 us
    reduce_scatter x1, waiting for transfers between devices, local(): summed = lax.psum_scatter(terms, 'seq', scatter_dimension=0, tiled=True)  49.3 us
    all_to_all x1, blocking collectives, local(): lax.all_to_all(outgoing, 'ep', split_axis=0, concat_axis=0, tiled=True)  33.6 us
    dot_general x1, matrix products, expert_terms(): return jnp.dot(hidden, down_matrix, preferred_element_type=jnp.float32)  16 us
    all_gather x1, blocking collectives, local(): older_rot = lax.all_gather(cache_rope[0], 'seq', axis=1, tiled=True)  12.7 us
    all_to_all x1, starting transfers between devices, local(): lax.all_to_all(summed, 'ep', split_axis=0, concat_axis=0, tiled=True)  9.67 us
    all_to_all x1, starting transfers between devices, local(): lax.all_to_all(layer_own, 'seq', split_axis=1, concat_axis=0, tiled=True)  8.91 us
  transfers between devices with their start and end apart: 6, of which 5 were waited for; matrix products, arithmetic and copies ran while one was open for 3% of the time, Pallas kernels for 0%

commit v1 on v0

v1 whole, which is shorter than its diff:
```python
import jax
import jax.numpy as jnp
from jax import lax
from jax.experimental import pallas as pl
from jax.experimental.pallas import tpu as pltpu
from jax.sharding import PartitionSpec as P

softmax_scale = 192 ** (-0.5)
rope_base = 10000.0
MESH = pl.DeviceIdType.MESH
SEQ = 8
YS = 4
XS = 4
ZS = 8
EPS = XS * ZS
CAP = 2
ROWS = SEQ * CAP
CHUNKS = 4
CROWS = ROWS * EPS // CHUNKS
HALF = CROWS // 2
SLICE = 896
UNITS = 256
NEW = 32
LATPAD = 640


def rms_rows(values, gain):
    mean_sq = jnp.mean(values * values, axis=-1, keepdims=True)
    return values * lax.rsqrt(mean_sq + 1e-06) * gain


def rotate_pairs(values, positions):
    half = values.shape[-1] // 2
    steps = jnp.arange(half, dtype=jnp.float32) * 2.0 / values.shape[-1]
    freqs = rope_base ** (-steps)
    angle = positions.astype(jnp.float32)[:, None] * freqs[None, :]
    first = values[:, :half]
    second = values[:, half:]
    cosine = jnp.cos(angle)
    sine = jnp.sin(angle)
    return jnp.concatenate(
        [first * cosine - second * sine, second * cosine + first * sine], axis=-1
    )


def score_block(query_lat, query_rot, key_lat, key_rot_cols):
    lat_part = jnp.dot(query_lat, key_lat.T, preferred_element_type=jnp.float32)
    rot_part = jnp.dot(query_rot, key_rot_cols, preferred_element_type=jnp.float32)
    return (lat_part + rot_part) * softmax_scale


def slot_targets(routes, doc):
    new, top = routes.shape
    blocks = new // 4
    grouped = routes.reshape(blocks, 4, top)
    same = (grouped[:, :, :, None, None] == grouped[:, None, None, :, :]).any(axis=4)
    order = jnp.arange(4, dtype=jnp.int32)
    earlier = (order[None, :] < order[:, None])[None, :, None, :]
    ranks = jnp.sum((same & earlier).astype(jnp.int32), axis=3).reshape(new, top)
    far = (routes // ZS - doc // ZS + XS) % XS * ZS + (routes % ZS - doc % ZS + ZS) % ZS
    return far * ROWS + jnp.arange(new, dtype=jnp.int32)[:, None] // 4 * CAP + ranks


def moe_kernel(
    entering,
    gain,
    tgt_cols,
    tgt,
    gates,
    w_gate,
    w_up,
    w_down,
    w_latent,
    w_rope,
    layer_out,
    raw_out,
    snd,
    rcv,
    outb,
    rows_in,
    w_in,
    w_out,
    w_lat,
    w_rot,
    part,
    sib,
    half,
    whole,
    final,
    back,
    lat_snd,
    lat_rcv,
    w_sem,
    ent_s,
    ent_r,
    go_s,
    go_r,
    y_s,
    y_r,
    rs_s,
    rs_r,
    ret_s,
    ret_r,
    lat_s,
    lat_r,
):
    s = lax.axis_index("seq")
    e = lax.axis_index("ep")
    y = s // 2
    c = s % 2
    x = e // ZS
    z = e % ZS
    other = y * 2 + 1 - c

    def at_y(dy):
        return lax.rem(y + dy + YS, YS) * 2 + c

    def pair_y(dy):
        return lax.rem(y + dy + YS, YS) * 2 + 1 - c

    def ep_plus(off):
        return lax.rem(x + off // ZS, XS) * ZS + lax.rem(z + off % ZS, ZS)

    def ep_minus(off):
        return lax.rem(x - off // ZS + XS, XS) * ZS + lax.rem(z - off % ZS + ZS, ZS)

    barrier = pltpu.get_barrier_semaphore()
    for off in range(1, EPS):
        pl.semaphore_signal(
            barrier, inc=1, device_id={"seq": s, "ep": ep_plus(off)}, device_id_type=MESH
        )
    for j in range(1, SEQ):
        pl.semaphore_signal(
            barrier, inc=1, device_id={"seq": lax.rem(s + j, SEQ), "ep": e}, device_id_type=MESH
        )

    loads = []

    def load(source, target):
        copy = pltpu.make_async_copy(source, target, w_sem.at[len(loads)])
        copy.start()
        loads.append(copy)

    for j in range(SEQ):
        load(w_gate.at[pl.ds(j * SLICE, SLICE), :], w_in.at[j, :, pl.ds(0, UNITS)])
        load(w_up.at[pl.ds(j * SLICE, SLICE), :], w_in.at[j, :, pl.ds(UNITS, UNITS)])
        load(w_down.at[:, pl.ds(j * SLICE, SLICE)], w_out.at[j])
    load(w_latent, w_lat)
    load(w_rope, w_rot)

    values = entering[...].astype(jnp.float32)
    mean_sq = jnp.mean(values * values, axis=-1, keepdims=True)
    normed = values * lax.rsqrt(mean_sq + 1e-06) * gain[...]
    normed = normed.astype(jnp.bfloat16).astype(jnp.float32)
    for j in range(SEQ):
        snd[j, 0:4, :] = values[:, j * SLICE : (j + 1) * SLICE]
        snd[j, 4:8, :] = normed[:, j * SLICE : (j + 1) * SLICE]
    pl.semaphore_wait(barrier, EPS - 1 + SEQ - 1)

    sends = []

    def remote(source, target, send_sem, recv_sem, seq, ep):
        return pltpu.make_async_remote_copy(
            src_ref=source,
            dst_ref=target,
            send_sem=send_sem,
            recv_sem=recv_sem,
            device_id={"seq": seq, "ep": ep},
            device_id_type=MESH,
        )

    def send(*args):
        copy = remote(*args)
        copy.start()
        sends.append(copy)

    def arrive(target, send_sem, recv_sem):
        remote(target, target, send_sem, recv_sem, other, e).wait_recv()

    for j in range(1, SEQ):
        to = lax.rem(s + j, SEQ)
        send(snd.at[to], rcv.at[s], ent_s.at[j], ent_r.at[j], to, e)
    rcv[s] = snd[s]
    for j in range(1, SEQ):
        arrive(rcv.at[lax.rem(s - j + SEQ, SEQ)], ent_s.at[j], ent_r.at[j])

    tokens = rcv[...].reshape(SEQ * 8, SLICE).astype(jnp.bfloat16)
    for k in range(CHUNKS):
        slots = lax.broadcasted_iota(jnp.int32, (CROWS, SEQ * 8), 0) + k * CROWS
        hit = slots == tgt_cols[0:1, :]
        for r in range(1, 8):
            hit = hit | (slots == tgt_cols[r : r + 1, :])
        place = jnp.where(hit, 1.0, 0.0).astype(jnp.bfloat16)
        outb[k * CROWS : (k + 1) * CROWS, :] = jnp.dot(
            place, tokens, preferred_element_type=jnp.float32
        ).astype(jnp.bfloat16)
        for off in range(k * EPS // CHUNKS, (k + 1) * EPS // CHUNKS):
            here = pl.ds(off * ROWS, ROWS)
            if off == 0:
                rows_in[s, here, :] = outb[here, :]
            else:
                send(
                    outb.at[here],
                    rows_in.at[s, here],
                    go_s.at[off],
                    go_r.at[off],
                    s,
                    ep_plus(off),
                )

    def rows(k):
        return pl.ds(k * CROWS, CROWS)

    def low(k):
        return pl.ds(k * CROWS, HALF)

    def high(k):
        return pl.ds(k * CROWS + HALF, HALF)

    def y_send(k, i, slice_at, which, to):
        ref = rows_in.at[slice_at, which]
        send(ref, ref, y_s.at[k, i], y_r.at[k, i], to, e)

    def y_arrive(k, i, slice_at, which):
        arrive(rows_in.at[slice_at, which], y_s.at[k, i], y_r.at[k, i])

    def gather_own(k):
        for off in range(k * EPS // CHUNKS, (k + 1) * EPS // CHUNKS):
            if off:
                arrive(rows_in.at[s, pl.ds(off * ROWS, ROWS)], go_s.at[off], go_r.at[off])
        y_send(k, 0, s, rows(k), at_y(1))
        y_send(k, 1, s, rows(k), at_y(-1))
        y_send(k, 2, s, rows(k), other)

    def gather_next(k):
        y_arrive(k, 0, at_y(-1), rows(k))
        y_send(k, 3, at_y(-1), low(k), at_y(1))
        y_send(k, 4, at_y(-1), rows(k), other)
        y_arrive(k, 1, at_y(1), rows(k))
        y_send(k, 5, at_y(1), high(k), at_y(-1))
        y_send(k, 6, at_y(1), rows(k), other)

    def gather_far(k):
        y_arrive(k, 3, at_y(2), low(k))
        y_arrive(k, 5, at_y(2), high(k))
        y_send(k, 7, at_y(2), rows(k), other)

    def compute(k):
        y_arrive(k, 2, other, rows(k))
        y_arrive(k, 4, pair_y(-1), rows(k))
        y_arrive(k, 6, pair_y(1), rows(k))
        y_arrive(k, 7, pair_y(2), rows(k))
        if k == 0:
            for copy in loads:
                copy.wait()

        def add(j, total):
            return total + jnp.dot(
                rows_in[j, rows(k), :], w_in[j], preferred_element_type=jnp.float32
            )

        total = lax.fori_loop(0, SEQ, add, jnp.zeros((CROWS, 2 * UNITS), jnp.float32))
        gate = total[:, :UNITS]
        hidden = (gate / (1.0 + jnp.exp(-gate)) * total[:, UNITS:]).astype(jnp.bfloat16)

        def down(j, carry):
            part[k, j] = jnp.dot(
                hidden, w_out[j], preferred_element_type=jnp.float32
            ).astype(jnp.bfloat16)
            return carry

        lax.fori_loop(0, SEQ, down, 0)
        for dy in (2, 1, 3, 0):
            send(
                part.at[k, pair_y(dy)], sib.at[k, dy], rs_s.at[k, dy], rs_r.at[k, dy], other, e
            )

    def plus(a, b):
        return (a.astype(jnp.float32) + b.astype(jnp.float32)).astype(jnp.bfloat16)

    def scatter_far(k):
        for dy in (2, 1, 3, 0):
            arrive(sib.at[k, dy], rs_s.at[k, dy], rs_r.at[k, dy])
            part[k, at_y(dy)] = plus(part[k, at_y(dy)], sib[k, dy])
            if dy == 2:
                far = part.at[k, at_y(2)]
                send(
                    far.at[pl.ds(0, HALF)],
                    half.at[k, 0],
                    rs_s.at[k, 4],
                    rs_r.at[k, 4],
                    at_y(1),
                    e,
                )
                send(
                    far.at[pl.ds(HALF, HALF)],
                    half.at[k, 1],
                    rs_s.at[k, 5],
                    rs_r.at[k, 5],
                    at_y(-1),
                    e,
                )

    def scatter_next(k):
        arrive(half.at[k, 0], rs_s.at[k, 4], rs_r.at[k, 4])
        part[k, at_y(1), 0:HALF, :] = plus(part[k, at_y(1), 0:HALF, :], half[k, 0])
        send(part.at[k, at_y(1)], whole.at[k, 0], rs_s.at[k, 6], rs_r.at[k, 6], at_y(1), e)
        arrive(half.at[k, 1], rs_s.at[k, 5], rs_r.at[k, 5])
        part[k, at_y(-1), HALF:CROWS, :] = plus(part[k, at_y(-1), HALF:CROWS, :], half[k, 1])
        send(part.at[k, at_y(-1)], whole.at[k, 1], rs_s.at[k, 7], rs_r.at[k, 7], at_y(-1), e)

    def give_back(k):
        arrive(whole.at[k, 0], rs_s.at[k, 6], rs_r.at[k, 6])
        arrive(whole.at[k, 1], rs_s.at[k, 7], rs_r.at[k, 7])
        final[k] = (
            part[k, s].astype(jnp.float32)
            + whole[k, 0].astype(jnp.float32)
            + whole[k, 1].astype(jnp.float32)
        ).astype(jnp.bfloat16)
        first = k * EPS // CHUNKS
        for off in range(first, (k + 1) * EPS // CHUNKS):
            here = pl.ds((off - first) * ROWS, ROWS)
            there = pl.ds(off * ROWS, ROWS)
            if off == 0:
                back[there, :] = final[k, here, :]
            else:
                send(
                    final.at[k, here],
                    back.at[there],
                    ret_s.at[off],
                    ret_r.at[off],
                    s,
                    ep_minus(off),
                )

    stages = (gather_own, gather_next, gather_far, compute, scatter_far, scatter_next, give_back)
    for step in range(CHUNKS + len(stages) - 1):
        for i in reversed(range(len(stages))):
            if 0 <= step - i < CHUNKS:
                stages[i](step - i)

    token = lax.broadcasted_iota(jnp.int32, (NEW, SEQ * 8), 0)
    column = lax.broadcasted_iota(jnp.int32, (NEW, SEQ * 8), 1)
    own = jnp.where(column == token // 4 * 8 + token % 4, 1.0, 0.0).astype(jnp.bfloat16)
    layer = jnp.dot(own, tokens, preferred_element_type=jnp.float32)
    for k in range(CHUNKS):
        slots = lax.broadcasted_iota(jnp.int32, (NEW, CROWS), 1) + k * CROWS
        share = jnp.zeros((NEW, CROWS), jnp.float32)
        for r in range(8):
            share = share + jnp.where(slots == tgt[:, r : r + 1], gates[:, r : r + 1], 0.0)
        share_high = share.astype(jnp.bfloat16)
        share_low = (share - share_high.astype(jnp.float32)).astype(jnp.bfloat16)
        for off in range(k * EPS // CHUNKS, (k + 1) * EPS // CHUNKS):
            if off:
                arrive(back.at[pl.ds(off * ROWS, ROWS)], ret_s.at[off], ret_r.at[off])
        values = back[k * CROWS : (k + 1) * CROWS, :]
        layer = layer + jnp.dot(share_high, values, preferred_element_type=jnp.float32)
        layer = layer + jnp.dot(share_low, values, preferred_element_type=jnp.float32)
    layer = layer.astype(jnp.bfloat16)
    layer_out[...] = layer
    lat_snd[:, 0:512] = jnp.dot(
        layer, w_lat[...], preferred_element_type=jnp.float32
    ).astype(jnp.bfloat16)
    rot = lax.dot_general(
        layer, w_rot[...], (((1,), (1,)), ((), ())), preferred_element_type=jnp.float32
    ).astype(jnp.bfloat16)
    lat_snd[:, 512:LATPAD] = jnp.concatenate([rot, jnp.zeros_like(rot)], axis=1)
    for j in range(1, SEQ):
        to = lax.rem(s + j, SEQ)
        send(lat_snd, lat_rcv.at[s], lat_s.at[j], lat_r.at[j], to, e)
    raw = lat_snd[...].astype(jnp.float32)
    for j in range(1, SEQ):
        place = lax.rem(s - j + SEQ, SEQ)
        arrive(lat_rcv.at[place], lat_s.at[j], lat_r.at[j])
        raw = raw + lat_rcv[place].astype(jnp.float32)
    raw_out[...] = raw
    for copy in sends:
        copy.wait_send()


def routed_layer(entering, gain, tgt_cols, tgt, gates, w_gate, w_up, w_down, w_latent, w_rope):
    bf = jnp.bfloat16
    dma = pltpu.SemaphoreType.DMA
    vmem = pl.BlockSpec(memory_space=pltpu.VMEM)
    hbm = pl.BlockSpec(memory_space=pl.ANY)
    return pl.pallas_call(
        moe_kernel,
        out_shape=(
            jax.ShapeDtypeStruct((NEW, SLICE), bf),
            jax.ShapeDtypeStruct((NEW, LATPAD), jnp.float32),
        ),
        in_specs=[vmem] * 5 + [hbm] * 5,
        out_specs=(vmem, vmem),
        scratch_shapes=[
            pltpu.VMEM((SEQ, 8, SLICE), jnp.float32),
            pltpu.VMEM((SEQ, 8, SLICE), jnp.float32),
            pltpu.VMEM((EPS * ROWS, SLICE), bf),
            pltpu.VMEM((SEQ, EPS * ROWS, SLICE), bf),
            pltpu.VMEM((SEQ, SLICE, 2 * UNITS), bf),
            pltpu.VMEM((SEQ, UNITS, SLICE), bf),
            pltpu.VMEM((SLICE, 512), bf),
            pltpu.VMEM((64, SLICE), bf),
            pltpu.VMEM((CHUNKS, SEQ, CROWS, SLICE), bf),
            pltpu.VMEM((CHUNKS, YS, CROWS, SLICE), bf),
            pltpu.VMEM((CHUNKS, 2, HALF, SLICE), bf),
            pltpu.VMEM((CHUNKS, 2, CROWS, SLICE), bf),
            pltpu.VMEM((CHUNKS, CROWS, SLICE), bf),
            pltpu.VMEM((EPS * ROWS, SLICE), bf),
            pltpu.VMEM((NEW, LATPAD), bf),
            pltpu.VMEM((SEQ, NEW, LATPAD), bf),
            dma((3 * SEQ + 2,)),
            dma((SEQ,)),
            dma((SEQ,)),
            dma((EPS,)),
            dma((EPS,)),
            dma((CHUNKS, 8)),
            dma((CHUNKS, 8)),
            dma((CHUNKS, 8)),
            dma((CHUNKS, 8)),
            dma((EPS,)),
            dma((EPS,)),
            dma((SEQ,)),
            dma((SEQ,)),
        ],
        compiler_params=pltpu.CompilerParams(
            collective_id=0, has_side_effects=True, vmem_limit_bytes=56 * 2**20
        ),
        cost_estimate=pl.CostEstimate(
            flops=6_000_000_000, bytes_accessed=14_000_000, transcendentals=131072
        ),
    )(entering, gain, tgt_cols, tgt, gates, w_gate, w_up, w_down, w_latent, w_rope)


def local(
    entering,
    moe_gain,
    expert_ids,
    gate_weights,
    w_gate,
    w_up,
    w_down,
    w_latent,
    w_rope,
    latent_gain,
    prefix_len,
    cache_latent,
    cache_rope,
    query_latent,
    query_rope,
):
    seq_count = lax.axis_size("seq")
    seq_place = lax.axis_index("seq")
    own_entering = entering[0]
    new_dev, width = own_entering.shape
    new = new_dev * seq_count
    prefix = prefix_len[0]
    heads = query_latent.shape[2] // cache_latent.shape[2]
    lat_width = cache_latent.shape[2]
    rot_width = cache_rope.shape[1]

    routes = expert_ids[0]
    tgt = slot_targets(routes, lax.axis_index("ep"))
    spaced = jnp.concatenate(
        [jnp.full((SEQ, 4, 8), -1, jnp.int32), tgt.reshape(SEQ, 4, 8)], axis=1
    )
    layer, raw = routed_layer(
        own_entering,
        moe_gain.reshape(1, width),
        spaced.reshape(SEQ * 8, 8).T,
        tgt,
        gate_weights[0],
        w_gate[0],
        w_up[0],
        w_down[0],
        w_latent,
        w_rope,
    )

    older_lat = lax.all_gather(cache_latent[0], "seq", axis=0, tiled=True)
    older_rot = lax.all_gather(cache_rope[0], "seq", axis=1, tiled=True)
    query_lat = query_latent[0].reshape(new_dev * heads, lat_width)
    query_rot = query_rope[0].reshape(new_dev * heads, rot_width)
    older = score_block(query_lat, query_rot, older_lat, older_rot)
    cache_ok = (jnp.arange(older_lat.shape[0], dtype=jnp.int32) < prefix)[None, :]
    older = jnp.where(cache_ok, older, -jnp.inf)
    older_high = jnp.max(older, axis=1)
    older_weights = jnp.exp(older - older_high[:, None])
    older_total = jnp.sum(older_weights, axis=1)
    older_sum = jnp.dot(
        older_weights.astype(jnp.bfloat16), older_lat, preferred_element_type=jnp.float32
    )

    fresh_lat = rms_rows(raw[:, :lat_width], latent_gain).astype(jnp.bfloat16)
    positions = prefix + jnp.arange(new, dtype=jnp.int32)
    fresh_rot = rotate_pairs(raw[:, lat_width : lat_width + rot_width], positions).astype(jnp.bfloat16)

    fresh = score_block(query_lat, query_rot, fresh_lat, fresh_rot.T)
    query_place = seq_place * new_dev + jnp.arange(new_dev * heads, dtype=jnp.int32) // heads
    fresh_ok = jnp.arange(new, dtype=jnp.int32)[None, :] <= query_place[:, None]
    fresh = jnp.where(fresh_ok, fresh, -jnp.inf)
    highest = jnp.maximum(older_high, jnp.max(fresh, axis=1))
    scale = jnp.exp(older_high - highest)
    fresh_weights = jnp.exp(fresh - highest[:, None])
    total = older_total * scale + jnp.sum(fresh_weights, axis=1)
    gathered = older_sum * scale[:, None] + jnp.dot(
        fresh_weights.astype(jnp.bfloat16), fresh_lat, preferred_element_type=jnp.float32
    )
    output = (gathered / total[:, None]).astype(jnp.bfloat16).reshape(new_dev, heads * lat_width)
    return (layer[None], output[None])


def solution(mesh):
    placed = (
        P("ep", "seq", None),
        P(),
        P("ep", None, None),
        P("ep", None, None),
        P("ep", None, "seq"),
        P("ep", None, "seq"),
        P("ep", "seq", None),
        P("seq", None),
        P(None, "seq"),
        P(),
        P("ep"),
        P("ep", "seq", None),
        P("ep", None, "seq"),
        P("ep", "seq", None),
        P("ep", "seq", None),
    )
    return jax.shard_map(
        local,
        mesh=mesh,
        in_specs=placed,
        out_specs=(P("ep", None, "seq"), P("ep", "seq", None)),
        check_vma=False,
    )
```

time: 292 us -> 157 us (0.54)
  waiting for transfers between devices: 159 us -> 0.7 us
  Pallas kernels: 0 us -> 113 us
  blocking collectives: 46.3 us -> 11.6 us
  matrix products: 35.8 us -> 4.93 us
  starting transfers between devices: 18.9 us -> 0.04 us
  local copies, waits for them, and re-layouts: 10.8 us -> 6.18 us
    pallas_call x0 -> x1, Pallas kernels: none -> 113 us  [routed_layer(): pl.pallas_call(moe_kernel, out_shape=(jax.ShapeDtypeStruct((NEW, SLICE),...]
    psum x1 -> x0, waiting for transfers between devices: 53.4 us -> none  [local(): raw = lax.psum(jnp.concatenate([latent_part, rope_part], axis=1), 'seq')]
    all_gather x1 -> x0, waiting for transfers between devices: 49.3 us -> none  [local(): lax.all_gather(arrived.reshape(total_slots, width), 'seq', axis=0, tiled=...]
    reduce_scatter x1 -> x0, waiting for transfers between devices: 49.3 us -> none  [local(): summed = lax.psum_scatter(terms, 'seq', scatter_dimension=0, tiled=True)]
    all_to_all x1 -> x0, blocking collectives: 33.6 us -> none  [local(): lax.all_to_all(outgoing, 'ep', split_axis=0, concat_axis=0, tiled=True)]
    dot_general x6 -> x0, matrix products: 26.7 us -> none  [the longest x1 16 us: expert_terms(): return jnp.dot(hidden, down_matrix, preferred_element_type=jnp.float32)]
    all_to_all x2 -> x0, starting transfers between devices: 18.6 us -> none  [the longest x1 9.67 us: local(): lax.all_to_all(summed, 'ep', split_axis=0, concat_axis=0, tiled=True)]
    all_to_all x2 -> x0, waiting for transfers between devices: 6.3 us -> none  [the longest x1 4.17 us: local(): lax.all_to_all(summed, 'ep', split_axis=0, concat_axis=0, tiled=True)]
  transfers between devices with their start and end apart: 6 -> 1, of which waited for: 5 -> 0; matrix products, arithmetic and copies ran while one was open for 3% -> 7% of each run, Pallas kernels for 0% -> 72%
where the time goes in v1:
time: 157 us
  Pallas kernels  113 us (72%)
  between operations  14.9 us (9%)
  blocking collectives  11.6 us (7%)
  local copies, waits for them, and re-layouts  6.18 us (4%)
  other arithmetic  5.74 us (4%)
  matrix products  4.93 us (3%)
    pallas_call x1, Pallas kernels, routed_layer(): pl.pallas_call(moe_kernel, out_shape=(jax.ShapeDtypeStruct((NEW, SLICE),...  113 us
    all_gather x1, blocking collectives, local(): older_rot = lax.all_gather(cache_rope[0], 'seq', axis=1, tiled=True)  11.6 us
    unnamed x18, local copies, waits for them, and re-layouts  3.67 us
    dot_general x2, matrix products, score_block(): lat_part = jnp.dot(query_lat, key_lat.T, preferred_element_type=jnp.float32)  3.16 us
  transfers between devices with their start and end apart: 1, of which 0 were waited for; matrix products, arithmetic and copies ran while one was open for 7% of the time, Pallas kernels for 72%

profile of v1, /device:TPU:1, one launch (start us, length us, event | category | flops | bytes accessed | tf_op | source)
XLA Modules:
  0.0 157.0 jit_solution(1293750324413379844)
XLA Ops:
  7.2 0.0 all-gather.4.cloned.1.call-start
  7.2 0.7 all-gather.4.cloned.1.call-update
  8.0 0.8 copy.30
  8.7 2.4 %compare_reduce_fusion = pred[8,4,8,4]{2,3,1,0:T(4,128)(4,1)S(1)} fusion(s32[8,4,8]{2,1,0:T(4,128)S(1)} %bitcast.51), kind=kLoop, calls=%fused_computation.15 | loop fusion | flops 15360 | bytes 2048 | tf_op jit(solution)/shard_map/reduce_or | solution.py:56
  11.1 0.1 convert_reduce_fusion
  11.2 0.1 fusion.32
  11.3 0.1 copy.41
  11.4 0.1 concatenate.7.clone
  11.5 0.7 reshape.137
  12.2 1.4 copy.39
  13.5 0.7 fusion.43.tgt
  14.2 0.0 copy-start.3
  14.2 0.0 copy-start.1
  14.2 0.0 copy-start.5
  14.2 0.0 copy-start.6
  14.2 113.0 %shard_map.158 = (bf16[32,896]{1,0:T(8,128)(2,1)}, f32[32,640]{1,0:T(8,128)}) custom-call(bf16[4,7168]{1,0:T(4,128)(2,1)} %bitcast.60, f32[1,7168]{1,0:T(1,128)} %bitcast.61, s32[8,64]{1,0:T(8,128)} %bitcast.56, s32[32,8]{1,0:T(8,128)} %fusion.43.tgt, f32[32,8]{1,0:T(8,128)} %bitcast.55, bf16[7168,256]{1,0:T(8,128)(2,1)} %bitcast.57, ...), custom_call_target="tpu_custom_call" | custom-call | flops 6000000000 | bytes 14000000 | tf_op jit(solution)/shard_map/pallas_call | solution.py:386
  127.9 0.0 copy-done.3
  127.9 0.2 reshape_squeeze.7
  128.1 0.0 copy-done.1
  128.1 0.4 reshape_squeeze.6
  128.5 0.0 copy-done.5
  128.5 11.6 %all-gather.1 = bf16[1,64,1024]{2,1,0:T(8,128)(2,1)S(1)} all-gather(bf16[1,64,128]{2,1,0:T(8,128)(2,1)S(1)} %copy-done.5), channel_id=3, replica_groups=mesh['seq'=8,'ep'=32] {'seq'}, dimensions={2}, use_global_device_ids=true | all-gather | bytes 147456 | tf_op jit(solution)/shard_map/all_gather | solution.py:480
  140.1 1.0 multiply_reduce_fusion
  141.1 0.9 fusion.22
  142.0 0.0 copy-done.6
  142.0 1.1 fusion.61
  143.1 0.2 fusion.63
  143.4 0.4 fusion.11
  143.8 0.0 all-gather.4.cloned.1.call-done
  143.8 2.1 %fusion.62 = (f32[512]{0:T(512)S(1)}, f32[512,1024]{1,0:T(8,128)S(1)}) fusion(f32[512,1024]{1,0:T(8,128)S(1)} %fusion.11, bf16[512,512]{1,0:T(8,128)(2,1)S(1)} %reshape_squeeze.6, bf16[1,1024,512]{2,1,0:T(8,128)(2,1)} %all-gather.4.cloned.1.call-done, pred[1024]{0:T(1024)(128)(4,1)S(1)} %iota_compare_fusion.1), kind=kOutput, calls=%fused_computation.117 | convolution fusion | flops 538967552 | bytes 5770240 | tf_op jit(solution)/shard_map/dot_general | solution.py:47
  145.9 0.0 copy-start
  145.9 0.5 fusion
  146.5 0.7 copy-done
  147.1 0.0 copy-start.2
  147.1 0.8 convolution_multiply_fusion
  147.9 0.1 copy-done.2
  148.0 0.0 copy-start.4
  148.0 0.3 fusion.3
  148.4 1.2 broadcast_in_dim_reshape.3
  149.5 0.0 copy-done.4
  149.5 0.6 copy.46
  (11 shorter events, 0.1 us)
Async XLA Ops:
  7.2 136.6 %all-gather.4.cloned.1.call-start = ((), (), s32[]{:S(2)}) async-start(), calls=%async_computation | async-start | bytes 1179648 | tf_op jit(solution)/shard_map/all_gather | solution.py:479
  14.2 113.7 %copy-start.3 = (bf16[1,4,8192]{2,1,0:T(4,128)(2,1)S(1)}, bf16[1,4,8192]{2,1,0:T(4,128)(2,1)}, u32[]{:S(2)}) copy-start(bf16[1,4,8192]{2,1,0:T(4,128)(2,1)} %param.29) | copy-start | bytes 196612
  14.2 113.8 %copy-start.1 = (bf16[1,4,65536]{2,1,0:T(4,128)(2,1)S(1)}, bf16[1,4,65536]{2,1,0:T(4,128)(2,1)}, u32[]{:S(2)}) copy-start(bf16[1,4,65536]{2,1,0:T(4,128)(2,1)} %param.28) | copy-start | bytes 1572868
  14.2 114.3 %copy-start.5 = (bf16[1,64,128]{2,1,0:T(8,128)(2,1)S(1)}, bf16[1,64,128]{2,1,0:T(8,128)(2,1)}, u32[]{:S(2)}) copy-start(bf16[1,64,128]{2,1,0:T(8,128)(2,1)} %param.27) | copy-start | bytes 49156
  14.2 127.8 %copy-start.6 = (f32[512]{0:T(512)S(1)}, f32[512]{0:T(512)}, u32[]{:S(2)}) copy-start(f32[512]{0:T(512)} %param.24) | copy-start | bytes 6148
  145.9 1.2 copy-start
  147.1 0.9 copy-start.2
  148.0 1.5 copy-start.4
Sparse Core Ops, SparseCore 0:
  9.9 31.0 all-gather.3

commit v2 on v1

v2 whole, which is shorter than its diff:
```python
import math

import jax
import jax.numpy as jnp
from jax import lax
from jax.experimental import pallas as pl
from jax.experimental.pallas import tpu as pltpu
from jax.sharding import PartitionSpec as P

softmax_scale = 192 ** (-0.5)
rope_base = 10000.0
MESH = pl.DeviceIdType.MESH
SEQ = 8
YS = 4
XS = 4
ZS = 8
EPS = XS * ZS
CAP = 2
ROWS = SEQ * CAP
PAIRS = ((0, 1), (6, 3), (5, 4), (7, 2))
SPOT = {dz: 2 * k + p for k, pair in enumerate(PAIRS) for p, dz in enumerate(pair)}
CHUNKS = len(PAIRS)
CROWS = ROWS * EPS // CHUNKS
XROWS = CROWS // XS
SLICE = 896
UNITS = 256
NEW = 32
LATPAD = 640
TOP = 8
HEADS = 128
LAT = 512
ROPE = 64
CACHE = 1024
KEYS = CACHE // SEQ


def moe_kernel(
    entering,
    gain,
    ids,
    gates,
    w_gate,
    w_up,
    w_down,
    w_latent,
    w_rope,
    latent_gain,
    prefix,
    cache_lat,
    cache_rot,
    query_lat,
    query_rot,
    layer_out,
    att_out,
    idbuf,
    info,
    info_in,
    snd,
    rcv,
    zs,
    zin,
    share_hi,
    share_lo,
    xs,
    rows_in,
    w_in,
    w_out,
    w_lat,
    w_rot,
    part,
    sib,
    whole,
    final,
    xback,
    zsum,
    zback,
    far_snd,
    far_rcv,
    lat_snd,
    lat_rcv,
    key_lat,
    key_rot,
    old_high,
    old_total,
    old_sum,
    w_sem,
    info_s,
    info_r,
    ent_s,
    ent_r,
    z_s,
    z_r,
    x_s,
    x_r,
    y_s,
    y_r,
    rs_s,
    rs_r,
    xb_s,
    xb_r,
    zb_s,
    zb_r,
    lat_s,
    lat_r,
    key_s,
    key_r,
):
    s = lax.axis_index("seq")
    e = lax.axis_index("ep")
    y = s // 2
    c = s % 2
    x = e // ZS
    z = e % ZS
    other = y * 2 + 1 - c

    def at_y(dy):
        return lax.rem(y + dy + YS, YS) * 2 + c

    def pair_y(dy):
        return lax.rem(y + dy + YS, YS) * 2 + 1 - c

    def at_z(dz):
        return x * ZS + lax.rem(z + dz + ZS, ZS)

    def at_x(dx):
        return lax.rem(x + dx + XS, XS) * ZS + z

    barrier = pltpu.get_barrier_semaphore()

    def greet(seq, ep):
        pl.semaphore_signal(
            barrier, inc=1, device_id={"seq": seq, "ep": ep}, device_id_type=MESH
        )

    for j in range(1, SEQ):
        greet(lax.rem(s + j, SEQ), e)
    for j in range(1, ZS):
        greet(s, at_z(j))
    for j in range(1, XS):
        greet(s, at_x(j))

    loads = []

    def load(source, target):
        copy = pltpu.make_async_copy(source, target, w_sem.at[len(loads)])
        copy.start()
        loads.append(copy)

    for j in range(SEQ):
        load(w_gate.at[pl.ds(j * SLICE, SLICE), :], w_in.at[j, :, pl.ds(0, UNITS)])
        load(w_up.at[pl.ds(j * SLICE, SLICE), :], w_in.at[j, :, pl.ds(UNITS, UNITS)])
        load(w_down.at[:, pl.ds(j * SLICE, SLICE)], w_out.at[j])
    load(w_latent, w_lat)
    load(w_rope, w_rot)

    values = entering[...].astype(jnp.float32)
    mean_sq = jnp.mean(values * values, axis=-1, keepdims=True)
    normed = values * lax.rsqrt(mean_sq + 1e-06) * gain[...]
    for j in range(SEQ):
        far = (j + SEQ // 2) % SEQ
        mine = normed[:, j * SLICE : (j + 1) * SLICE]
        snd[j] = jnp.concatenate(
            [
                values[:, j * SLICE : (j + 1) * SLICE],
                mine,
                normed[:, far * SLICE : (far + 1) * SLICE],
                jnp.zeros_like(mine),
            ],
            axis=0,
        ).astype(jnp.bfloat16)

    idbuf[...] = jnp.full((TOP, 128), -1, jnp.int32)
    idbuf[:, 0:NEW] = ids[...]
    routes = idbuf[...]
    lane = lax.broadcasted_iota(jnp.int32, (TOP, 128), 1)
    rank = jnp.zeros((TOP, 128), jnp.int32)
    for i in range(1, 4):
        earlier = pltpu.roll(routes, i, 1)
        for r in range(TOP):
            same = (routes == earlier[r : r + 1, :]) & (lane % 4 >= i)
            rank = rank + same.astype(jnp.int32)
    code = ((routes % ZS - z + ZS) % ZS) * (XS * ROWS) + ((routes // ZS - x + XS) % XS) * ROWS
    code = code + lane // 4 * CAP + rank
    info[0:TOP, :] = code.astype(jnp.float32)
    info[TOP : 2 * TOP, :] = jnp.zeros((TOP, 128), jnp.float32)
    info[TOP : 2 * TOP, 0:NEW] = gates[...]
    pl.semaphore_wait(barrier, SEQ - 1 + ZS - 1 + XS - 1)

    sends = []

    def remote(source, target, send_sem, recv_sem, seq, ep):
        return pltpu.make_async_remote_copy(
            src_ref=source,
            dst_ref=target,
            send_sem=send_sem,
            recv_sem=recv_sem,
            device_id={"seq": seq, "ep": ep},
            device_id_type=MESH,
        )

    def send(*args):
        copy = remote(*args)
        copy.start()
        sends.append(copy)

    def arrive(target, send_sem, recv_sem):
        remote(target, target, send_sem, recv_sem, other, e).wait_recv()

    for j in range(1, SEQ):
        to = lax.rem(s + j, SEQ)
        send(snd.at[to], rcv.at[s], ent_s.at[j], ent_r.at[j], to, e)
    rcv[s] = snd[s]
    info_in[0] = info[...]
    for k in range(CHUNKS):
        for p in range(2):
            spot = 2 * k + p
            if spot:
                send(
                    info,
                    info_in.at[spot],
                    info_s.at[spot],
                    info_r.at[spot],
                    s,
                    at_z(PAIRS[k][p]),
                )

    def key_refs(place):
        return (
            key_lat.at[pl.ds(place * KEYS, KEYS)],
            key_rot.at[:, pl.ds(place * KEYS, KEYS)],
        )

    key_lat[pl.ds(s * KEYS, KEYS), :] = cache_lat[...]
    key_rot[:, pl.ds(s * KEYS, KEYS)] = cache_rot[...]

    def key_send(n, place, to):
        for i, ref in enumerate(key_refs(place)):
            send(ref, ref, key_s.at[n, i], key_r.at[n, i], to, e)

    def key_arrive(n, place):
        for i, ref in enumerate(key_refs(place)):
            arrive(ref, key_s.at[n, i], key_r.at[n, i])

    for j in range(1, SEQ):
        arrive(rcv.at[lax.rem(s - j + SEQ, SEQ)], ent_s.at[j], ent_r.at[j])

    tokens = rcv[...].reshape(SEQ * 16, SLICE)

    def pick(first):
        token = lax.broadcasted_iota(jnp.int32, (NEW, SEQ * 16), 0)
        column = lax.broadcasted_iota(jnp.int32, (NEW, SEQ * 16), 1)
        chosen = column == token // 4 * 16 + token % 4 + first
        return jnp.dot(
            jnp.where(chosen, 1.0, 0.0).astype(jnp.bfloat16),
            tokens,
            preferred_element_type=jnp.float32,
        )

    for i in range(2):
        zs[i] = pick(4 + 4 * i).astype(jnp.bfloat16)

    def z_send(i, dz, ref, way):
        spot = SPOT[dz]
        send(ref, zin.at[i, spot], z_s.at[i, spot], z_r.at[i, spot], s, at_z(way))

    def z_pass(i, dz, way):
        z_send(i, (dz + way) % ZS, zin.at[i, SPOT[dz]], way)

    for i in range(2):
        z_send(i, 1, zs.at[i], 1)
        z_send(i, ZS - 1, zs.at[i], -1)
        zin[i, 0] = zs[i]
    for n, to in enumerate((at_y(1), at_y(-1), at_y(2), other)):
        key_send(n, s, to)

    def relay(hop):
        for i in range(2):
            for dz, way in ((hop, 1), (ZS - hop, -1)):
                if hop < ZS // 2:
                    arrive(zin.at[i, SPOT[dz]], z_s.at[i, SPOT[dz]], z_r.at[i, SPOT[dz]])
                    if hop < ZS // 2 - 1 or (i == 0) == (way == 1):
                        z_pass(i, dz, way)
            if hop == ZS // 2:
                arrive(zin.at[i, SPOT[hop]], z_s.at[i, SPOT[hop]], z_r.at[i, SPOT[hop]])

    def keys_on(unused):
        for n, dy in ((0, -1), (1, 1), (2, 2)):
            key_arrive(n, at_y(dy))
            key_send(4 + n, at_y(dy), other)

    slices = (s, at_y(2))

    def rows(k):
        return pl.ds(k * CROWS, CROWS)

    def routed(k):
        codes, shares = [], []
        for p in range(2):
            spot = 2 * k + p
            if spot:
                arrive(info_in.at[spot], info_s.at[spot], info_r.at[spot])
            local = info_in[spot, 0:TOP, 0:NEW] - float(PAIRS[k][p] * XS * ROWS)
            inside = (local >= 0.0) & (local < float(XS * ROWS))
            row = local + jnp.floor(local * (1.0 / ROWS)) * ROWS + float(p * ROWS)
            codes.append(jnp.where(inside, row, -1.0))
            shares.append(info_in[spot, TOP : 2 * TOP, 0:NEW])
        code = jnp.concatenate(codes, axis=1)
        share = jnp.concatenate(shares, axis=1)
        at = lax.broadcasted_iota(jnp.int32, (CROWS, 2 * NEW), 0).astype(jnp.float32)
        place = jnp.zeros((CROWS, 2 * NEW), jnp.float32)
        weigh = jnp.zeros((CROWS, 2 * NEW), jnp.float32)
        for r in range(TOP):
            hit = at == code[r : r + 1, :]
            place = place + jnp.where(hit, 1.0, 0.0)
            weigh = weigh + jnp.where(hit, share[r : r + 1, :], 0.0)
        place = place.astype(jnp.bfloat16)
        high = weigh.astype(jnp.bfloat16)
        share_hi[k] = high
        share_lo[k] = (weigh - high.astype(jnp.float32)).astype(jnp.bfloat16)
        for i in range(2):
            both = zin[i, 2 * k : 2 * k + 2].reshape(2 * NEW, SLICE)
            xs[i, k] = jnp.dot(place, both, preferred_element_type=jnp.float32).astype(
                jnp.bfloat16
            )
            for dx in (1, 3, 2):
                send(
                    xs.at[i, k, pl.ds(dx * XROWS, XROWS)],
                    rows_in.at[slices[i], pl.ds(k * CROWS + dx * XROWS, XROWS)],
                    x_s.at[k, i, dx],
                    x_r.at[k, i, dx],
                    s,
                    at_x(dx),
                )
            rows_in[slices[i], pl.ds(k * CROWS, XROWS), :] = xs[i, k, 0:XROWS, :]

    def y_send(k, i, slice_at, to):
        ref = rows_in.at[slice_at, rows(k)]
        send(ref, ref, y_s.at[k, i], y_r.at[k, i], to, e)

    def y_arrive(k, i, slice_at):
        arrive(rows_in.at[slice_at, rows(k)], y_s.at[k, i], y_r.at[k, i])

    def gather_own(k):
        for i in range(2):
            for dx in (1, 3, 2):
                arrive(
                    rows_in.at[slices[i], pl.ds(k * CROWS + dx * XROWS, XROWS)],
                    x_s.at[k, i, dx],
                    x_r.at[k, i, dx],
                )
            if i == 0:
                y_send(k, 0, s, at_y(1))
                y_send(k, 1, s, at_y(-1))
                y_send(k, 2, s, other)
            else:
                y_send(k, 3, slices[1], other)

    def gather_next(k):
        y_arrive(k, 0, at_y(-1))
        y_send(k, 4, at_y(-1), other)
        y_arrive(k, 1, at_y(1))
        y_send(k, 5, at_y(1), other)

    def compute(k):
        y_arrive(k, 2, other)
        y_arrive(k, 3, pair_y(2))
        y_arrive(k, 4, pair_y(-1))
        y_arrive(k, 5, pair_y(1))
        if k == 0:
            for copy in loads:
                copy.wait()

        def add(j, total):
            return total + jnp.dot(
                rows_in[j, rows(k), :], w_in[j], preferred_element_type=jnp.float32
            )

        total = lax.fori_loop(0, SEQ, add, jnp.zeros((CROWS, 2 * UNITS), jnp.float32))
        gate = total[:, :UNITS]
        hidden = (gate / (1.0 + jnp.exp(-gate)) * total[:, UNITS:]).astype(jnp.bfloat16)

        def down(j, carry):
            part[k, j] = jnp.dot(
                hidden, w_out[j], preferred_element_type=jnp.float32
            ).astype(jnp.bfloat16)
            return carry

        lax.fori_loop(0, SEQ, down, 0)
        for dy in (1, 3, 2, 0):
            send(
                part.at[k, pair_y(dy)], sib.at[k, dy], rs_s.at[k, dy], rs_r.at[k, dy], other, e
            )

    def plus(a, b):
        return (a.astype(jnp.float32) + b.astype(jnp.float32)).astype(jnp.bfloat16)

    def x_return(k, i):
        for dx in (1, 3, 2):
            send(
                final.at[k, i, pl.ds(dx * XROWS, XROWS)],
                xback.at[i, k, pl.ds(dx * XROWS, XROWS)],
                xb_s.at[k, i, dx],
                xb_r.at[k, i, dx],
                s,
                at_x(-dx),
            )
        xback[i, k, 0:XROWS, :] = final[k, i, 0:XROWS, :]

    def scatter_pair(k):
        for i, dy in ((0, 1), (1, 3)):
            arrive(sib.at[k, dy], rs_s.at[k, dy], rs_r.at[k, dy])
            part[k, at_y(dy)] = plus(part[k, at_y(dy)], sib[k, dy])
            send(
                part.at[k, at_y(dy)],
                whole.at[k, i],
                rs_s.at[k, 4 + i],
                rs_r.at[k, 4 + i],
                at_y(dy),
                e,
            )
        arrive(sib.at[k, 2], rs_s.at[k, 2], rs_r.at[k, 2])
        final[k, 1] = plus(part[k, at_y(2)], sib[k, 2])
        x_return(k, 1)
        arrive(sib.at[k, 0], rs_s.at[k, 0], rs_r.at[k, 0])

    def give_back(k):
        arrive(whole.at[k, 0], rs_s.at[k, 4], rs_r.at[k, 4])
        arrive(whole.at[k, 1], rs_s.at[k, 5], rs_r.at[k, 5])
        final[k, 0] = (
            part[k, s].astype(jnp.float32)
            + sib[k, 0].astype(jnp.float32)
            + whole[k, 0].astype(jnp.float32)
            + whole[k, 1].astype(jnp.float32)
        ).astype(jnp.bfloat16)
        x_return(k, 0)

    def weigh_back(k):
        for i in (1, 0):
            for dx in (1, 3, 2):
                arrive(
                    xback.at[i, k, pl.ds(dx * XROWS, XROWS)],
                    xb_s.at[k, i, dx],
                    xb_r.at[k, i, dx],
                )
            got = xback[i, k]
            over = (((0,), (0,)), ((), ()))
            summed = lax.dot_general(
                share_hi[k], got, over, preferred_element_type=jnp.float32
            ) + lax.dot_general(share_lo[k], got, over, preferred_element_type=jnp.float32)
            zsum[i, 2 * k : 2 * k + 2] = summed.astype(jnp.bfloat16).reshape(2, NEW, SLICE)
            for p in range(2):
                spot = 2 * k + p
                if spot:
                    send(
                        zsum.at[i, spot],
                        zback.at[i, spot],
                        zb_s.at[i, spot],
                        zb_r.at[i, spot],
                        s,
                        at_z(-PAIRS[k][p]),
                    )
                else:
                    zback[i, 0] = zsum[i, 0]

    def scores(b, keys, rot_keys, turned):
        here = slice(b * HEADS, (b + 1) * HEADS)
        over = (((1,), (1,)), ((), ()))
        lat_part = lax.dot_general(
            query_lat[here, :], keys, over, preferred_element_type=jnp.float32
        )
        if turned:
            rot_part = lax.dot_general(
                query_rot[here, :], rot_keys, over, preferred_element_type=jnp.float32
            )
        else:
            rot_part = jnp.dot(query_rot[here, :], rot_keys, preferred_element_type=jnp.float32)
        return (lat_part + rot_part) * softmax_scale

    def cached(b):
        if b == 0:
            for n, dy in ((3, 0), (4, -1), (5, 1), (6, 2)):
                key_arrive(n, pair_y(dy))
        here = slice(b * HEADS, (b + 1) * HEADS)
        older = scores(b, key_lat[...], key_rot[...], False)
        place = lax.broadcasted_iota(jnp.int32, (HEADS, CACHE), 1)
        older = jnp.where(place < prefix[0, 0], older, -jnp.inf)
        high = jnp.max(older, axis=1, keepdims=True)
        weights = jnp.exp(older - high)
        old_high[here, :] = high
        old_total[here, :] = jnp.sum(weights, axis=1, keepdims=True)
        old_sum[here, :] = jnp.dot(
            weights.astype(jnp.bfloat16), key_lat[...], preferred_element_type=jnp.float32
        )

    own, nxt, comp, pair, give, weigh = (
        gather_own,
        gather_next,
        compute,
        scatter_pair,
        give_back,
        weigh_back,
    )
    schedule = (
        ((relay, 1), (routed, 0), (relay, 2), (relay, 3), (routed, 1), (own, 0), (relay, 4))
        + ((routed, 2), (nxt, 0), (own, 1), (routed, 3), (keys_on, 0))
        + ((comp, 0), (nxt, 1), (own, 2), (cached, 0), (pair, 0), (comp, 1), (nxt, 2), (own, 3))
        + ((cached, 1), (give, 0), (pair, 1), (comp, 2), (nxt, 3), (cached, 2))
        + ((weigh, 0), (give, 1), (pair, 2), (comp, 3), (cached, 3))
        + ((weigh, 1), (give, 2), (pair, 3), (weigh, 2), (give, 3), (weigh, 3))
    )
    for stage, k in schedule:
        stage(k)

    def collect(i):
        total = zback[i, 0].astype(jnp.float32)
        for spot in range(1, ZS):
            arrive(zback.at[i, spot], zb_s.at[i, spot], zb_r.at[i, spot])
            total = total + zback[i, spot].astype(jnp.float32)
        return total

    index = lax.broadcasted_iota(jnp.int32, (NEW, ROPE // 2), 1).astype(jnp.float32)
    position = lax.broadcasted_iota(jnp.int32, (NEW, ROPE // 2), 0) + prefix[0, 0]
    angle = position.astype(jnp.float32) * jnp.exp(index * (-2.0 / ROPE * math.log(rope_base)))
    cosine = jnp.cos(angle)
    sine = jnp.sin(angle)
    far_snd[...] = collect(1).astype(jnp.bfloat16)
    send(far_snd, far_rcv, lat_s.at[0], lat_r.at[0], slices[1], e)
    layer = pick(0) + collect(0)
    arrive(far_rcv, lat_s.at[0], lat_r.at[0])
    layer = (layer + far_rcv[...].astype(jnp.float32)).astype(jnp.bfloat16)
    layer_out[...] = layer
    lat_snd[:, 0:LAT] = jnp.dot(
        layer, w_lat[...], preferred_element_type=jnp.float32
    ).astype(jnp.bfloat16)
    rot = lax.dot_general(
        layer, w_rot[...], (((1,), (1,)), ((), ())), preferred_element_type=jnp.float32
    ).astype(jnp.bfloat16)
    lat_snd[:, LAT:LATPAD] = jnp.concatenate([rot, jnp.zeros_like(rot)], axis=1)
    for j in range(1, SEQ):
        to = lax.rem(s + j, SEQ)
        send(lat_snd, lat_rcv.at[s], lat_s.at[j], lat_r.at[j], to, e)
    raw = lat_snd[...].astype(jnp.float32)
    for j in range(1, SEQ):
        place = lax.rem(s - j + SEQ, SEQ)
        arrive(lat_rcv.at[place], lat_s.at[j], lat_r.at[j])
        raw = raw + lat_rcv[place].astype(jnp.float32)
    fresh = raw[:, 0:LAT]
    fresh_sq = jnp.mean(fresh * fresh, axis=-1, keepdims=True)
    fresh = (fresh * lax.rsqrt(fresh_sq + 1e-06) * latent_gain[...]).astype(jnp.bfloat16)
    first = raw[:, LAT : LAT + ROPE // 2]
    second = raw[:, LAT + ROPE // 2 : LAT + ROPE]
    rotated = jnp.concatenate(
        [first * cosine - second * sine, second * cosine + first * sine], axis=1
    ).astype(jnp.bfloat16)
    for b in range(4):
        here = slice(b * HEADS, (b + 1) * HEADS)
        newer = scores(b, fresh, rotated, True)
        place = lax.broadcasted_iota(jnp.int32, (HEADS, NEW), 1)
        newer = jnp.where(place <= s * 4 + b, newer, -jnp.inf)
        high = jnp.maximum(old_high[here, :], jnp.max(newer, axis=1, keepdims=True))
        scale = jnp.exp(old_high[here, :] - high)
        weights = jnp.exp(newer - high)
        total = old_total[here, :] * scale + jnp.sum(weights, axis=1, keepdims=True)
        summed = old_sum[here, :] * scale + jnp.dot(
            weights.astype(jnp.bfloat16), fresh, preferred_element_type=jnp.float32
        )
        att_out[here, :] = (summed / total).astype(jnp.bfloat16)
    for copy in sends:
        copy.wait_send()


def block(*arrays):
    bf = jnp.bfloat16
    f32 = jnp.float32
    dma = pltpu.SemaphoreType.DMA
    vmem = pl.BlockSpec(memory_space=pltpu.VMEM)
    hbm = pl.BlockSpec(memory_space=pl.ANY)
    return pl.pallas_call(
        moe_kernel,
        out_shape=(
            jax.ShapeDtypeStruct((NEW, SLICE), bf),
            jax.ShapeDtypeStruct((4 * HEADS, LAT), bf),
        ),
        in_specs=[vmem] * 4
        + [hbm] * 5
        + [vmem, pl.BlockSpec(memory_space=pltpu.SMEM)]
        + [vmem] * 4,
        out_specs=(vmem, vmem),
        scratch_shapes=[
            pltpu.VMEM((TOP, 128), jnp.int32),
            pltpu.VMEM((2 * TOP, 128), f32),
            pltpu.VMEM((ZS, 2 * TOP, 128), f32),
            pltpu.VMEM((SEQ, 16, SLICE), bf),
            pltpu.VMEM((SEQ, 16, SLICE), bf),
            pltpu.VMEM((2, NEW, SLICE), bf),
            pltpu.VMEM((2, ZS, NEW, SLICE), bf),
            pltpu.VMEM((CHUNKS, CROWS, 2 * NEW), bf),
            pltpu.VMEM((CHUNKS, CROWS, 2 * NEW), bf),
            pltpu.VMEM((2, CHUNKS, CROWS, SLICE), bf),
            pltpu.VMEM((SEQ, EPS * ROWS, SLICE), bf),
            pltpu.VMEM((SEQ, SLICE, 2 * UNITS), bf),
            pltpu.VMEM((SEQ, UNITS, SLICE), bf),
            pltpu.VMEM((SLICE, 512), bf),
            pltpu.VMEM((64, SLICE), bf),
            pltpu.VMEM((CHUNKS, SEQ, CROWS, SLICE), bf),
            pltpu.VMEM((CHUNKS, YS, CROWS, SLICE), bf),
            pltpu.VMEM((CHUNKS, 2, CROWS, SLICE), bf),
            pltpu.VMEM((CHUNKS, 2, CROWS, SLICE), bf),
            pltpu.VMEM((2, CHUNKS, CROWS, SLICE), bf),
            pltpu.VMEM((2, ZS, NEW, SLICE), bf),
            pltpu.VMEM((2, ZS, NEW, SLICE), bf),
            pltpu.VMEM((NEW, SLICE), bf),
            pltpu.VMEM((NEW, SLICE), bf),
            pltpu.VMEM((NEW, LATPAD), bf),
            pltpu.VMEM((SEQ, NEW, LATPAD), bf),
            pltpu.VMEM((CACHE, LAT), bf),
            pltpu.VMEM((ROPE, CACHE), bf),
            pltpu.VMEM((4 * HEADS, 1), f32),
            pltpu.VMEM((4 * HEADS, 1), f32),
            pltpu.VMEM((4 * HEADS, LAT), f32),
            dma((3 * SEQ + 2,)),
            dma((ZS,)),
            dma((ZS,)),
            dma((SEQ,)),
            dma((SEQ,)),
            dma((2, ZS)),
            dma((2, ZS)),
            dma((CHUNKS, 2, XS)),
            dma((CHUNKS, 2, XS)),
            dma((CHUNKS, 6)),
            dma((CHUNKS, 6)),
            dma((CHUNKS, 6)),
            dma((CHUNKS, 6)),
            dma((CHUNKS, 2, XS)),
            dma((CHUNKS, 2, XS)),
            dma((2, ZS)),
            dma((2, ZS)),
            dma((SEQ,)),
            dma((SEQ,)),
            dma((7, 2)),
            dma((7, 2)),
        ],
        compiler_params=pltpu.CompilerParams(
            collective_id=0, has_side_effects=True, vmem_limit_bytes=56 * 2**20
        ),
        cost_estimate=pl.CostEstimate(
            flops=6_000_000_000, bytes_accessed=14_000_000, transcendentals=131072
        ),
    )(*arrays)


def local(
    entering,
    moe_gain,
    expert_ids,
    gate_weights,
    w_gate,
    w_up,
    w_down,
    w_latent,
    w_rope,
    latent_gain,
    prefix_len,
    cache_latent,
    cache_rope,
    query_latent,
    query_rope,
):
    layer, output = block(
        entering[0],
        moe_gain.reshape(1, -1),
        expert_ids[0].T,
        gate_weights[0].T,
        w_gate[0],
        w_up[0],
        w_down[0],
        w_latent,
        w_rope,
        latent_gain.reshape(1, LAT),
        prefix_len.reshape(1, 1),
        cache_latent[0],
        cache_rope[0],
        query_latent.reshape(4 * HEADS, LAT),
        query_rope.reshape(4 * HEADS, ROPE),
    )
    return (layer[None], output.reshape(1, 4, HEADS * LAT))


def solution(mesh):
    placed = (
        P("ep", "seq", None),
        P(),
        P("ep", None, None),
        P("ep", None, None),
        P("ep", None, "seq"),
        P("ep", None, "seq"),
        P("ep", "seq", None),
        P("seq", None),
        P(None, "seq"),
        P(),
        P("ep"),
        P("ep", "seq", None),
        P("ep", None, "seq"),
        P("ep", "seq", None),
        P("ep", "seq", None),
    )
    return jax.shard_map(
        local,
        mesh=mesh,
        in_specs=placed,
        out_specs=(P("ep", None, "seq"), P("ep", "seq", None)),
        check_vma=False,
    )
```

time: 157 us -> 115 us (0.73)
  between operations: 14.9 us -> 1.29 us
  blocking collectives: 11.6 us -> 0 us
  Pallas kernels: 113 us -> 106 us
  other arithmetic: 5.74 us -> 0 us
  matrix products: 4.93 us -> 0 us
    all_gather x1 -> x0, blocking collectives: 11.6 us -> none  [local(): older_rot = lax.all_gather(cache_rope[0], 'seq', axis=1, tiled=True)]
    pallas_call x1, Pallas kernels: 113 us -> 106 us  [block(): pl.pallas_call(moe_kernel, out_shape=(jax.ShapeDtypeStruct((NEW, SLICE),...]
    reshape x1 -> x3, local copies, waits for them, and re-layouts: 0.67 us -> 6.13 us  [the longest x1 2.25 us: local(): query_latent.reshape(4 * HEADS, LAT)]
    dot_general x6 -> x0, matrix products: 4.93 us -> none  [the longest x2 3.16 us: score_block(): lat_part = jnp.dot(query_lat, key_lat.T, preferred_element_type=jnp.float32)]
    reduce_or x1 -> x0, other arithmetic: 2.35 us -> none  [slot_targets(): (grouped[:, :, :, None, None] == grouped[:, None, None, :, :]).any(axis=4)]
    unnamed x18 -> x1, local copies, waits for them, and re-layouts: 3.67 us -> 1.45 us
    another operation x3 -> x0, local copies, waits for them, and re-layouts: 1.76 us -> none  [the longest x1 1.18 us: local(): return (layer[None], output[None])]
    reduce_sum x4 -> x0, other arithmetic: 1.62 us -> none  [the longest x1 0.95 us: rms_rows(): mean_sq = jnp.mean(values * values, axis=-1, keepdims=True)]
  transfers between devices with their start and end apart: 1 -> 0, of which waited for: 0 -> 0; matrix products, arithmetic and copies ran while one was open for 7% -> 0% of each run, Pallas kernels for 72% -> 0%
where the time goes in v2:
time: 115 us
  Pallas kernels  106 us (92%)
  local copies, waits for them, and re-layouts  7.58 us (7%)
  between operations  1.29 us (1%)
    pallas_call x1, Pallas kernels, block(): pl.pallas_call(moe_kernel, out_shape=(jax.ShapeDtypeStruct((NEW, SLICE),...  106 us

profile of v2, /device:TPU:1, one launch (start us, length us, event | category | flops | bytes accessed | tf_op | source)
XLA Modules:
  0.0 114.7 jit_solution(15567560347845027463)
XLA Ops:
  1.3 1.7 %reshape.26.query_rot = bf16[512,64]{1,0:T(8,128)(2,1)} reshape(bf16[1,4,8192]{2,1,0:T(4,128)(2,1)} %param.29) | data formatting | bytes 131072 | tf_op jit(solution)/shard_map/reshape | solution.py:684
  2.9 2.2 %reshape.25.query_lat = bf16[512,512]{1,0:T(8,128)(2,1)} reshape(bf16[1,4,65536]{2,1,0:T(4,128)(2,1)} %param.28) | data formatting | bytes 1048576 | tf_op jit(solution)/shard_map/reshape | solution.py:683
  5.2 105.9 %shard_map.158 = (bf16[32,896]{1,0:T(8,128)(2,1)}, bf16[512,512]{1,0:T(8,128)(2,1)}) custom-call(bf16[4,7168]{1,0:T(4,128)(2,1)} %bitcast.22, f32[1,7168]{1,0:T(1,128)} %bitcast.23, s32[8,32]{1,0:T(8,128)} %bitcast.25, f32[8,32]{1,0:T(8,128)} %bitcast.26, bf16[7168,256]{1,0:T(8,128)(2,1)} %bitcast.18, bf16[7168,256]{1,0:T(8,128)(2,1)} %bitcast.19, ...), custom_call_target="tpu_custom_call" | custom-call | flops 6000000000 | bytes 14000000 | tf_op jit(solution)/shard_map/pallas_call | solution.py:578
  111.1 2.2 %reshape.27 = bf16[1,4,65536]{2,1,0:T(4,128)(2,1)} reshape(bf16[512,512]{1,0:T(8,128)(2,1)} %get-tuple-element.5) | data formatting | bytes 1048576 | tf_op jit(solution)/shard_map/reshape | solution.py:686
  113.3 1.4 %copy.19 = bf16[1,32,896]{2,1,0:T(8,128)(2,1)} copy(bf16[1,32,896]{2,1,0:T(8,128)(2,1)} %bitcast.17) | data formatting | bytes 114688

commit v3 on v2

--- a/solution.py
+++ b/solution.py
@@ -18,7 +18,8 @@
 CAP = 2
 ROWS = SEQ * CAP
 PAIRS = ((0, 1), (6, 3), (5, 4), (7, 2))
-SPOT = {dz: 2 * k + p for k, pair in enumerate(PAIRS) for p, dz in enumerate(pair)}
+GROUP = len(PAIRS[0])
+SPOT = {dz: GROUP * k + p for k, pair in enumerate(PAIRS) for p, dz in enumerate(pair)}
 CHUNKS = len(PAIRS)
 CROWS = ROWS * EPS // CHUNKS
 XROWS = CROWS // XS
@@ -59,6 +60,7 @@
     rcv,
     zs,
     zin,
+    places,
     share_hi,
     share_lo,
     xs,
@@ -80,6 +82,9 @@
     lat_rcv,
     key_lat,
     key_rot,
+    turned_lat,
+    turned_rot,
+    zero_rot,
     old_high,
     old_total,
     old_sum,
@@ -212,8 +217,8 @@
     rcv[s] = snd[s]
     info_in[0] = info[...]
     for k in range(CHUNKS):
-        for p in range(2):
-            spot = 2 * k + p
+        for p in range(GROUP):
+            spot = GROUP * k + p
             if spot:
                 send(
                     info,
@@ -233,6 +238,28 @@
     key_lat[pl.ds(s * KEYS, KEYS), :] = cache_lat[...]
     key_rot[:, pl.ds(s * KEYS, KEYS)] = cache_rot[...]
 
+    def turn(g, carry):
+        for odd in range(2):
+            pieces = []
+            for i in range(4):
+                at = ((g * 4 + i) * 2 + odd) * LAT
+                piece = query_lat[0:4, pl.ds(pl.multiple_of(at, LAT), LAT)]
+                pieces.append(piece.astype(jnp.float32))
+            at = pl.multiple_of(odd * 2 * HEADS + g * 16, 16)
+            turned_lat[pl.ds(at, 16), :] = jnp.concatenate(pieces, axis=0).astype(jnp.bfloat16)
+        pieces = []
+        for i in range(4):
+            at = pl.multiple_of((g * 4 + i) * 2 * ROPE, 2 * ROPE)
+            pieces.append(query_rot[0:4, pl.ds(at, 2 * ROPE)].astype(jnp.float32))
+        at = pl.multiple_of(g * 16, 16)
+        turned_rot[pl.ds(at, 16), :] = jnp.concatenate(pieces, axis=0).astype(jnp.bfloat16)
+        return carry
+
+    def queries(n):
+        if n == 0:
+            zero_rot[...] = jnp.zeros_like(zero_rot)
+        lax.fori_loop(4 * n, 4 * n + 4, turn, 0)
+
     def key_send(n, place, to):
         for i, ref in enumerate(key_refs(place)):
             send(ref, ref, key_s.at[n, i], key_r.at[n, i], to, e)
@@ -266,22 +293,33 @@
     def z_pass(i, dz, way):
         z_send(i, (dz + way) % ZS, zin.at[i, SPOT[dz]], way)
 
-    for i in range(2):
+    def z_start(i):
         z_send(i, 1, zs.at[i], 1)
         z_send(i, ZS - 1, zs.at[i], -1)
+
+    z_start(0)
+    for i in range(2):
         zin[i, 0] = zs[i]
     for n, to in enumerate((at_y(1), at_y(-1), at_y(2), other)):
         key_send(n, s, to)
 
+    def relays(i, hop):
+        for dz, way in ((hop, 1), (ZS - hop, -1)):
+            if hop < ZS // 2:
+                arrive(zin.at[i, SPOT[dz]], z_s.at[i, SPOT[dz]], z_r.at[i, SPOT[dz]])
+                if hop < ZS // 2 - 1 or (i == 0) == (way == 1):
+                    z_pass(i, dz, way)
+        if hop == ZS // 2:
+            arrive(zin.at[i, SPOT[hop]], z_s.at[i, SPOT[hop]], z_r.at[i, SPOT[hop]])
+
     def relay(hop):
-        for i in range(2):
-            for dz, way in ((hop, 1), (ZS - hop, -1)):
-                if hop < ZS // 2:
-                    arrive(zin.at[i, SPOT[dz]], z_s.at[i, SPOT[dz]], z_r.at[i, SPOT[dz]])
-                    if hop < ZS // 2 - 1 or (i == 0) == (way == 1):
-                        z_pass(i, dz, way)
-            if hop == ZS // 2:
-                arrive(zin.at[i, SPOT[hop]], z_s.at[i, SPOT[hop]], z_r.at[i, SPOT[hop]])
+        relays(0, hop)
+
+    def far_relay(hop):
+        if hop:
+            relays(1, hop)
+        else:
+            z_start(1)
 
     def keys_on(unused):
         for n, dy in ((0, -1), (1, 1), (2, 2)):
@@ -295,43 +333,48 @@
 
     def routed(k):
         codes, shares = [], []
-        for p in range(2):
-            spot = 2 * k + p
+        for p in range(GROUP):
+            spot = GROUP * k + p
             if spot:
                 arrive(info_in.at[spot], info_s.at[spot], info_r.at[spot])
             local = info_in[spot, 0:TOP, 0:NEW] - float(PAIRS[k][p] * XS * ROWS)
             inside = (local >= 0.0) & (local < float(XS * ROWS))
-            row = local + jnp.floor(local * (1.0 / ROWS)) * ROWS + float(p * ROWS)
+            row = local + jnp.floor(local * (1.0 / ROWS)) * ((GROUP - 1) * ROWS) + float(p * ROWS)
             codes.append(jnp.where(inside, row, -1.0))
             shares.append(info_in[spot, TOP : 2 * TOP, 0:NEW])
         code = jnp.concatenate(codes, axis=1)
         share = jnp.concatenate(shares, axis=1)
-        at = lax.broadcasted_iota(jnp.int32, (CROWS, 2 * NEW), 0).astype(jnp.float32)
-        place = jnp.zeros((CROWS, 2 * NEW), jnp.float32)
-        weigh = jnp.zeros((CROWS, 2 * NEW), jnp.float32)
+        at = lax.broadcasted_iota(jnp.int32, (CROWS, GROUP * NEW), 0).astype(jnp.float32)
+        place = jnp.zeros((CROWS, GROUP * NEW), jnp.float32)
+        weigh = jnp.zeros((CROWS, GROUP * NEW), jnp.float32)
         for r in range(TOP):
             hit = at == code[r : r + 1, :]
             place = place + jnp.where(hit, 1.0, 0.0)
             weigh = weigh + jnp.where(hit, share[r : r + 1, :], 0.0)
-        place = place.astype(jnp.bfloat16)
+        places[k] = place.astype(jnp.bfloat16)
         high = weigh.astype(jnp.bfloat16)
         share_hi[k] = high
         share_lo[k] = (weigh - high.astype(jnp.float32)).astype(jnp.bfloat16)
-        for i in range(2):
-            both = zin[i, 2 * k : 2 * k + 2].reshape(2 * NEW, SLICE)
-            xs[i, k] = jnp.dot(place, both, preferred_element_type=jnp.float32).astype(
-                jnp.bfloat16
+        x_go(k, 0)
+
+    def far_routed(k):
+        x_go(k, 1)
+
+    def x_go(k, i):
+        both = zin[i, GROUP * k : GROUP * (k + 1)].reshape(GROUP * NEW, SLICE)
+        xs[i, k] = jnp.dot(places[k], both, preferred_element_type=jnp.float32).astype(
+            jnp.bfloat16
+        )
+        for dx in (1, 3, 2):
+            send(
+                xs.at[i, k, pl.ds(dx * XROWS, XROWS)],
+                rows_in.at[slices[i], pl.ds(k * CROWS + dx * XROWS, XROWS)],
+                x_s.at[k, i, dx],
+                x_r.at[k, i, dx],
+                s,
+                at_x(dx),
             )
-            for dx in (1, 3, 2):
-                send(
-                    xs.at[i, k, pl.ds(dx * XROWS, XROWS)],
-                    rows_in.at[slices[i], pl.ds(k * CROWS + dx * XROWS, XROWS)],
-                    x_s.at[k, i, dx],
-                    x_r.at[k, i, dx],
-                    s,
-                    at_x(dx),
-                )
-            rows_in[slices[i], pl.ds(k * CROWS, XROWS), :] = xs[i, k, 0:XROWS, :]
+        rows_in[slices[i], pl.ds(k * CROWS, XROWS), :] = xs[i, k, 0:XROWS, :]
 
     def y_send(k, i, slice_at, to):
         ref = rows_in.at[slice_at, rows(k)]
@@ -340,20 +383,23 @@
     def y_arrive(k, i, slice_at):
         arrive(rows_in.at[slice_at, rows(k)], y_s.at[k, i], y_r.at[k, i])
 
+    def x_arrive(k, i):
+        for dx in (1, 3, 2):
+            arrive(
+                rows_in.at[slices[i], pl.ds(k * CROWS + dx * XROWS, XROWS)],
+                x_s.at[k, i, dx],
+                x_r.at[k, i, dx],
+            )
+
     def gather_own(k):
-        for i in range(2):
-            for dx in (1, 3, 2):
-                arrive(
-                    rows_in.at[slices[i], pl.ds(k * CROWS + dx * XROWS, XROWS)],
-                    x_s.at[k, i, dx],
-                    x_r.at[k, i, dx],
-                )
-            if i == 0:
-                y_send(k, 0, s, at_y(1))
-                y_send(k, 1, s, at_y(-1))
-                y_send(k, 2, s, other)
-            else:
-                y_send(k, 3, slices[1], other)
+        x_arrive(k, 0)
+        y_send(k, 0, s, at_y(1))
+        y_send(k, 1, s, at_y(-1))
+        y_send(k, 2, s, other)
+
+    def gather_far(k):
+        x_arrive(k, 1)
+        y_send(k, 3, slices[1], other)
 
     def gather_next(k):
         y_arrive(k, 0, at_y(-1))
@@ -447,9 +493,9 @@
             summed = lax.dot_general(
                 share_hi[k], got, over, preferred_element_type=jnp.float32
             ) + lax.dot_general(share_lo[k], got, over, preferred_element_type=jnp.float32)
-            zsum[i, 2 * k : 2 * k + 2] = summed.astype(jnp.bfloat16).reshape(2, NEW, SLICE)
-            for p in range(2):
-                spot = 2 * k + p
+            zsum[i, GROUP * k : GROUP * (k + 1)] = summed.astype(jnp.bfloat16).reshape(GROUP, NEW, SLICE)
+            for p in range(GROUP):
+                spot = GROUP * k + p
                 if spot:
                     send(
                         zsum.at[i, spot],
@@ -462,18 +508,20 @@
                 else:
                     zback[i, 0] = zsum[i, 0]
 
-    def scores(b, keys, rot_keys, turned):
-        here = slice(b * HEADS, (b + 1) * HEADS)
+    def scores(b, keys, rot_keys):
         over = (((1,), (1,)), ((), ()))
         lat_part = lax.dot_general(
-            query_lat[here, :], keys, over, preferred_element_type=jnp.float32
+            turned_lat[b * HEADS : (b + 1) * HEADS, :],
+            keys,
+            over,
+            preferred_element_type=jnp.float32,
         )
-        if turned:
-            rot_part = lax.dot_general(
-                query_rot[here, :], rot_keys, over, preferred_element_type=jnp.float32
-            )
-        else:
-            rot_part = jnp.dot(query_rot[here, :], rot_keys, preferred_element_type=jnp.float32)
+        half = b % 2
+        rot_part = jnp.dot(
+            turned_rot[half * HEADS : (half + 1) * HEADS, :],
+            rot_keys,
+            preferred_element_type=jnp.float32,
+        )
         return (lat_part + rot_part) * softmax_scale
 
     def cached(b):
@@ -481,7 +529,11 @@
             for n, dy in ((3, 0), (4, -1), (5, 1), (6, 2)):
                 key_arrive(n, pair_y(dy))
         here = slice(b * HEADS, (b + 1) * HEADS)
-        older = scores(b, key_lat[...], key_rot[...], False)
+        if b < 2:
+            rot_keys = jnp.concatenate([key_rot[...], zero_rot[...]], axis=0)
+        else:
+            rot_keys = jnp.concatenate([zero_rot[...], key_rot[...]], axis=0)
+        older = scores(b, key_lat[...], rot_keys)
         place = lax.broadcasted_iota(jnp.int32, (HEADS, CACHE), 1)
         older = jnp.where(place < prefix[0, 0], older, -jnp.inf)
         high = jnp.max(older, axis=1, keepdims=True)
@@ -501,12 +553,60 @@
         weigh_back,
     )
     schedule = (
-        ((relay, 1), (routed, 0), (relay, 2), (relay, 3), (routed, 1), (own, 0), (relay, 4))
-        + ((routed, 2), (nxt, 0), (own, 1), (routed, 3), (keys_on, 0))
-        + ((comp, 0), (nxt, 1), (own, 2), (cached, 0), (pair, 0), (comp, 1), (nxt, 2), (own, 3))
-        + ((cached, 1), (give, 0), (pair, 1), (comp, 2), (nxt, 3), (cached, 2))
-        + ((weigh, 0), (give, 1), (pair, 2), (comp, 3), (cached, 3))
-        + ((weigh, 1), (give, 2), (pair, 3), (weigh, 2), (give, 3), (weigh, 3))
+        (relay, 1),
+        (far_relay, 0),
+        (routed, 0),
+        (queries, 0),
+        (relay, 2),
+        (far_relay, 1),
+        (own, 0),
+        (relay, 3),
+        (far_routed, 0),
+        (routed, 1),
+        (queries, 1),
+        (far_relay, 2),
+        (keys_on, 0),
+        (relay, 4),
+        (far_relay, 3),
+        (gather_far, 0),
+        (queries, 2),
+        (nxt, 0),
+        (own, 1),
+        (far_routed, 1),
+        (routed, 2),
+        (far_relay, 4),
+        (queries, 3),
+        (comp, 0),
+        (gather_far, 1),
+        (nxt, 1),
+        (own, 2),
+        (far_routed, 2),
+        (routed, 3),
+        (pair, 0),
+        (cached, 0),
+        (comp, 1),
+        (gather_far, 2),
+        (nxt, 2),
+        (own, 3),
+        (far_routed, 3),
+        (give, 0),
+        (pair, 1),
+        (cached, 1),
+        (comp, 2),
+        (gather_far, 3),
+        (nxt, 3),
+        (weigh, 0),
+        (give, 1),
+        (pair, 2),
+        (cached, 2),
+        (comp, 3),
+        (weigh, 1),
+        (give, 2),
+        (pair, 3),
+        (cached, 3),
+        (weigh, 2),
+        (give, 3),
+        (weigh, 3),
     )
     for stage, k in schedule:
         stage(k)
@@ -539,6 +639,8 @@
     for j in range(1, SEQ):
         to = lax.rem(s + j, SEQ)
         send(lat_snd, lat_rcv.at[s], lat_s.at[j], lat_r.at[j], to, e)
+    for copy in sends[: 1 - SEQ]:
+        copy.wait_send()
     raw = lat_snd[...].astype(jnp.float32)
     for j in range(1, SEQ):
         place = lax.rem(s - j + SEQ, SEQ)
@@ -551,12 +653,15 @@
     second = raw[:, LAT + ROPE // 2 : LAT + ROPE]
     rotated = jnp.concatenate(
         [first * cosine - second * sine, second * cosine + first * sine], axis=1
-    ).astype(jnp.bfloat16)
+    ).T.astype(jnp.bfloat16)
     for b in range(4):
         here = slice(b * HEADS, (b + 1) * HEADS)
-        newer = scores(b, fresh, rotated, True)
+        blank = jnp.zeros((ROPE, NEW), jnp.bfloat16)
+        both = [rotated, blank] if b < 2 else [blank, rotated]
+        newer = scores(b, fresh, jnp.concatenate(both, axis=0))
         place = lax.broadcasted_iota(jnp.int32, (HEADS, NEW), 1)
-        newer = jnp.where(place <= s * 4 + b, newer, -jnp.inf)
+        asker = lax.broadcasted_iota(jnp.int32, (HEADS, NEW), 0) % 4 + s * 4
+        newer = jnp.where(place <= asker, newer, -jnp.inf)
         high = jnp.maximum(old_high[here, :], jnp.max(newer, axis=1, keepdims=True))
         scale = jnp.exp(old_high[here, :] - high)
         weights = jnp.exp(newer - high)
@@ -564,8 +669,13 @@
         summed = old_sum[here, :] * scale + jnp.dot(
             weights.astype(jnp.bfloat16), fresh, preferred_element_type=jnp.float32
         )
-        att_out[here, :] = (summed / total).astype(jnp.bfloat16)
-    for copy in sends:
+        result = summed * (1.0 / total)
+        for i in range(HEADS // 4):
+            head = (b % 2 * (HEADS // 4) + i) * 2 + b // 2
+            att_out[:, head * LAT : (head + 1) * LAT] = result[4 * i : 4 * i + 4, :].astype(
+                jnp.bfloat16
+            )
+    for copy in sends[1 - SEQ :]:
         copy.wait_send()
 
 
@@ -579,7 +689,7 @@
         moe_kernel,
         out_shape=(
             jax.ShapeDtypeStruct((NEW, SLICE), bf),
-            jax.ShapeDtypeStruct((4 * HEADS, LAT), bf),
+            jax.ShapeDtypeStruct((4, HEADS * LAT), bf),
         ),
         in_specs=[vmem] * 4
         + [hbm] * 5
@@ -594,8 +704,9 @@
             pltpu.VMEM((SEQ, 16, SLICE), bf),
             pltpu.VMEM((2, NEW, SLICE), bf),
             pltpu.VMEM((2, ZS, NEW, SLICE), bf),
-            pltpu.VMEM((CHUNKS, CROWS, 2 * NEW), bf),
-            pltpu.VMEM((CHUNKS, CROWS, 2 * NEW), bf),
+            pltpu.VMEM((CHUNKS, CROWS, GROUP * NEW), bf),
+            pltpu.VMEM((CHUNKS, CROWS, GROUP * NEW), bf),
+            pltpu.VMEM((CHUNKS, CROWS, GROUP * NEW), bf),
             pltpu.VMEM((2, CHUNKS, CROWS, SLICE), bf),
             pltpu.VMEM((SEQ, EPS * ROWS, SLICE), bf),
             pltpu.VMEM((SEQ, SLICE, 2 * UNITS), bf),
@@ -614,6 +725,9 @@
             pltpu.VMEM((NEW, LATPAD), bf),
             pltpu.VMEM((SEQ, NEW, LATPAD), bf),
             pltpu.VMEM((CACHE, LAT), bf),
+            pltpu.VMEM((ROPE, CACHE), bf),
+            pltpu.VMEM((4 * HEADS, LAT), bf),
+            pltpu.VMEM((2 * HEADS, 2 * ROPE), bf),
             pltpu.VMEM((ROPE, CACHE), bf),
             pltpu.VMEM((4 * HEADS, 1), f32),
             pltpu.VMEM((4 * HEADS, 1), f32),
@@ -680,10 +794,10 @@
         prefix_len.reshape(1, 1),
         cache_latent[0],
         cache_rope[0],
-        query_latent.reshape(4 * HEADS, LAT),
-        query_rope.reshape(4 * HEADS, ROPE),
+        query_latent[0],
+        query_rope[0],
     )
-    return (layer[None], output.reshape(1, 4, HEADS * LAT))
+    return (layer[None], output[None])
 
 
 def solution(mesh):

time: 115 us -> 108 us (0.939)
  local copies, waits for them, and re-layouts: 7.58 us -> 3.46 us
  Pallas kernels: 106 us -> 103 us
    reshape x3 -> x0, local copies, waits for them, and re-layouts: 6.13 us -> none  [the longest x1 2.25 us: local(): query_latent.reshape(4 * HEADS, LAT)]
    pallas_call x1, Pallas kernels: 106 us -> 103 us  [block(): pl.pallas_call(moe_kernel, out_shape=(jax.ShapeDtypeStruct((NEW, SLICE),...]
    unnamed x1 -> x2, local copies, waits for them, and re-layouts: 1.45 us -> 3.46 us
where the time goes in v3:
time: 108 us
  Pallas kernels  103 us (95%)
  local copies, waits for them, and re-layouts  3.46 us (3%)
  between operations  1.29 us (1%)
    pallas_call x1, Pallas kernels, block(): pl.pallas_call(moe_kernel, out_shape=(jax.ShapeDtypeStruct((NEW, SLICE),...  103 us
    unnamed x2, local copies, waits for them, and re-layouts  3.46 us

profile of v3, /device:TPU:1, one launch (start us, length us, event | category | flops | bytes accessed | tf_op | source)
XLA Modules:
  0.0 107.8 jit_solution(8603698103624597208)
XLA Ops:
  1.3 103.1 %shard_map.158 = (bf16[32,896]{1,0:T(8,128)(2,1)}, bf16[4,65536]{1,0:T(4,128)(2,1)}) custom-call(bf16[4,7168]{1,0:T(4,128)(2,1)} %bitcast.28, f32[1,7168]{1,0:T(1,128)} %bitcast.29, s32[8,32]{1,0:T(8,128)} %bitcast.31, f32[8,32]{1,0:T(8,128)} %bitcast.32, bf16[7168,256]{1,0:T(8,128)(2,1)} %bitcast.22, bf16[7168,256]{1,0:T(8,128)(2,1)} %bitcast.23, ...), custom_call_target="tpu_custom_call" | custom-call | flops 6000000000 | bytes 14000000 | tf_op jit(solution)/shard_map/pallas_call | solution.py:688
  104.3 1.4 %copy.20 = bf16[1,32,896]{2,1,0:T(8,128)(2,1)} copy(bf16[1,32,896]{2,1,0:T(8,128)(2,1)} %bitcast.21) | data formatting | bytes 114688
  105.8 2.0 %copy.21 = bf16[1,4,65536]{2,1,0:T(4,128)(2,1)} copy(bf16[1,4,65536]{2,1,0:T(4,128)(2,1)} %bitcast.20) | data formatting | bytes 1048576

commit v4 on v3

--- a/solution.py
+++ b/solution.py
@@ -17,7 +17,7 @@
 EPS = XS * ZS
 CAP = 2
 ROWS = SEQ * CAP
-PAIRS = ((0, 1), (6, 3), (5, 4), (7, 2))
+PAIRS = ((0, 1), (7, 2), (6, 3), (5, 4))
 GROUP = len(PAIRS[0])
 SPOT = {dz: GROUP * k + p for k, pair in enumerate(PAIRS) for p, dz in enumerate(pair)}
 CHUNKS = len(PAIRS)
@@ -70,6 +70,7 @@
     w_lat,
     w_rot,
     part,
+    sums,
     sib,
     whole,
     final,
@@ -407,35 +408,42 @@
         y_arrive(k, 1, at_y(1))
         y_send(k, 5, at_y(1), other)
 
+    def add_slices(k, parity, total):
+        def add(dy, total):
+            j = lax.rem(y + dy, YS) * 2 + parity
+            return total + jnp.dot(
+                rows_in[j, rows(k), :], w_in[j], preferred_element_type=jnp.float32
+            )
+
+        return lax.fori_loop(0, YS, add, total)
+
+    def early(k):
+        if k == 0:
+            for copy in loads:
+                copy.wait()
+        sums[k] = add_slices(k, c, jnp.zeros((CROWS, 2 * UNITS), jnp.float32))
+
     def compute(k):
         y_arrive(k, 2, other)
         y_arrive(k, 3, pair_y(2))
         y_arrive(k, 4, pair_y(-1))
         y_arrive(k, 5, pair_y(1))
-        if k == 0:
-            for copy in loads:
-                copy.wait()
-
-        def add(j, total):
-            return total + jnp.dot(
-                rows_in[j, rows(k), :], w_in[j], preferred_element_type=jnp.float32
-            )
-
-        total = lax.fori_loop(0, SEQ, add, jnp.zeros((CROWS, 2 * UNITS), jnp.float32))
+        total = add_slices(k, 1 - c, sums[k])
         gate = total[:, :UNITS]
         hidden = (gate / (1.0 + jnp.exp(-gate)) * total[:, UNITS:]).astype(jnp.bfloat16)
 
-        def down(j, carry):
+        def down(j):
             part[k, j] = jnp.dot(
                 hidden, w_out[j], preferred_element_type=jnp.float32
             ).astype(jnp.bfloat16)
-            return carry
-
-        lax.fori_loop(0, SEQ, down, 0)
+
         for dy in (1, 3, 2, 0):
+            down(pair_y(dy))
             send(
                 part.at[k, pair_y(dy)], sib.at[k, dy], rs_s.at[k, dy], rs_r.at[k, dy], other, e
             )
+        for dy in (1, 3, 2, 0):
+            down(at_y(dy))
 
     def plus(a, b):
         return (a.astype(jnp.float32) + b.astype(jnp.float32)).astype(jnp.bfloat16)
@@ -574,6 +582,7 @@
         (own, 1),
         (far_routed, 1),
         (routed, 2),
+        (early, 0),
         (far_relay, 4),
         (queries, 3),
         (comp, 0),
@@ -582,6 +591,7 @@
         (own, 2),
         (far_routed, 2),
         (routed, 3),
+        (early, 1),
         (pair, 0),
         (cached, 0),
         (comp, 1),
@@ -589,12 +599,14 @@
         (nxt, 2),
         (own, 3),
         (far_routed, 3),
+        (early, 2),
         (give, 0),
         (pair, 1),
         (cached, 1),
         (comp, 2),
         (gather_far, 3),
         (nxt, 3),
+        (early, 3),
         (weigh, 0),
         (give, 1),
         (pair, 2),
@@ -714,6 +726,7 @@
             pltpu.VMEM((SLICE, 512), bf),
             pltpu.VMEM((64, SLICE), bf),
             pltpu.VMEM((CHUNKS, SEQ, CROWS, SLICE), bf),
+            pltpu.VMEM((CHUNKS, CROWS, 2 * UNITS), f32),
             pltpu.VMEM((CHUNKS, YS, CROWS, SLICE), bf),
             pltpu.VMEM((CHUNKS, 2, CROWS, SLICE), bf),
             pltpu.VMEM((CHUNKS, 2, CROWS, SLICE), bf),

time: 108 us -> 103 us (0.954)
  Pallas kernels: 103 us -> 98.3 us
    pallas_call x1, Pallas kernels: 103 us -> 98.3 us  [block(): pl.pallas_call(moe_kernel, out_shape=(jax.ShapeDtypeStruct((NEW, SLICE),...]
where the time goes in v4:
time: 103 us
  Pallas kernels  98.3 us (95%)
  local copies, waits for them, and re-layouts  3.46 us (3%)
  between operations  1.29 us (1%)
    pallas_call x1, Pallas kernels, block(): pl.pallas_call(moe_kernel, out_shape=(jax.ShapeDtypeStruct((NEW, SLICE),...  98.3 us
    unnamed x2, local copies, waits for them, and re-layouts  3.46 us

profile of v4, /device:TPU:1, one launch (start us, length us, event | category | flops | bytes accessed | tf_op | source)
XLA Modules:
  0.0 103.1 jit_solution(4352312575106485668)
XLA Ops:
  1.3 98.3 %shard_map.158 = (bf16[32,896]{1,0:T(8,128)(2,1)}, bf16[4,65536]{1,0:T(4,128)(2,1)}) custom-call(bf16[4,7168]{1,0:T(4,128)(2,1)} %bitcast.28, f32[1,7168]{1,0:T(1,128)} %bitcast.29, s32[8,32]{1,0:T(8,128)} %bitcast.31, f32[8,32]{1,0:T(8,128)} %bitcast.32, bf16[7168,256]{1,0:T(8,128)(2,1)} %bitcast.22, bf16[7168,256]{1,0:T(8,128)(2,1)} %bitcast.23, ...), custom_call_target="tpu_custom_call" | custom-call | flops 6000000000 | bytes 14000000 | tf_op jit(solution)/shard_map/pallas_call | solution.py:700
  99.6 1.4 %copy.20 = bf16[1,32,896]{2,1,0:T(8,128)(2,1)} copy(bf16[1,32,896]{2,1,0:T(8,128)(2,1)} %bitcast.21) | data formatting | bytes 114688
  101.1 2.0 %copy.21 = bf16[1,4,65536]{2,1,0:T(4,128)(2,1)} copy(bf16[1,4,65536]{2,1,0:T(4,128)(2,1)} %bitcast.20) | data formatting | bytes 1048576
